TPU v7x, 32 devices: a whole 2x2x4 slice. The times are simulated.
32 devices in a mesh: fsdp: 8 (over z, core), grp: 2 (over y), tp: 2 (over x).
Axes of the slice: x: 2, y: 2, z: 4, core: 2. Of those that a mesh axis runs over, the one named last changes fastest.
Arguments:
- learn_in: bfloat16 [2752, 4096], P('fsdp', 'grp'), may hold values from -6 to 6
- learn_cot: bfloat16 [2752, 4096], P('fsdp', 'grp'), may hold values from -0.109375 to 0.109375
- preact: bfloat16 [2752, 2, 1536], P('fsdp', None, 'tp'), may hold values from -6 to 6
- hidden_cot: bfloat16 [2752, 1536], P('fsdp', 'tp'), may hold values from -0.109375 to 0.109375
- master: float32 [2, 2048, 3, 1536], P('grp', 'fsdp', None, 'tp'), may hold values from -0.09375 to 0.09375
- moment: float32 [2, 2048, 3, 1536], P('grp', 'fsdp', None, 'tp'), may hold values from -4 to 4
- second: float32 [2, 2048, 3, 1536], P('grp', 'fsdp', None, 'tp'), may hold values from 0.05 to 1
- rollout_in: bfloat16 [8192, 4096], P(('fsdp', 'grp'), 'tp'), may hold values from -6 to 6
- routes: int32 [8192, 8], P(('fsdp', 'grp')), may hold values from 0 to 127, as said below
- route_weight: float32 [8192, 8], P(('fsdp', 'grp')), may hold values from 0.05 to 0.6
Outputs:
- master_new: float32 [2, 2048, 3, 1536], P('grp', 'fsdp', None, 'tp')
- moment_new: float32 [2, 2048, 3, 1536], P('grp', 'fsdp', None, 'tp')
- second_new: float32 [2, 2048, 3, 1536], P('grp', 'fsdp', None, 'tp')
- expert_out: bfloat16 [8192, 4096], P(('fsdp', 'grp'), 'tp')
Inputs may be any that keep to these rules, and one draw needn't show every extreme that they name: `routes`: each row names 8 different experts. In each rollout group of 512 consecutive rows, expert 0 is named by at most 112 rows, and by exactly 112 rows in at least one group.
All inputs are finite; a program needn't handle non-finite values.
Results may differ from a plain program's by a relative error of at most 0.022.
Values may be sent and summed in bfloat16 or wider, within the bound.
No kernel may reach another device: no remote copies, remote signals or barrier semaphores. Data moves between devices by JAX's collectives and lax.ppermute only.
A program may use at most 128 MiB of HBM per device.

v0:
```python
import functools

import jax
import jax.numpy as jnp
from jax import lax
from jax.experimental import pallas as pl
from jax.experimental.pallas import tpu as pltpu
from jax.sharding import PartitionSpec as P

CAP = 112

first_decay = 0.9
second_decay = 0.95
first_fix = 1.0 - 0.9**10
second_fix = 1.0 - 0.95**10
learn_rate = 0.002
weight_decay = 0.1
epsilon = 1e-08

F32 = jnp.float32
BF16 = jnp.bfloat16
BY_TOKENS = (((0,), (0,)), ((), ()))
BY_LAST = (((1,), (1,)), ((), ()))

CORES = [(i, i ^ 1) for i in range(8)]
NEAR = [(i, i ^ 2) for i in range(8)]
FAR = [(i, i ^ 4) for i in range(8)]
SWAP = [(0, 1), (1, 0)]
TURN = [(0, 0), (1, 2), (2, 1), (3, 3)]
ROUND = [(0, 1), (1, 3), (3, 2), (2, 0)]


def activations(preact, hidden_cot):
    gate_pre = preact[:, 0, :].astype(F32)
    up_pre = preact[:, 1, :].astype(F32)
    logistic = jax.nn.sigmoid(gate_pre)
    activated = gate_pre * logistic
    hidden_act = (activated * up_pre).astype(BF16)
    cotangent = hidden_cot.astype(F32)
    grad_gate = (cotangent * up_pre * logistic * (1.0 + gate_pre * (1.0 - logistic))).astype(BF16)
    grad_up = (cotangent * activated).astype(BF16)
    return hidden_act, grad_gate, grad_up


def adam(master, moment, second, grad):
    moment_new = first_decay * moment + (1.0 - first_decay) * grad
    second_new = second_decay * second + (1.0 - second_decay) * grad * grad
    step_size = moment_new / first_fix / (jnp.sqrt(second_new / second_fix) + epsilon)
    master_new = master - learn_rate * (step_size + weight_decay * master)
    return master_new, moment_new, second_new


def slots(routes, route_weight):
    named = routes == 0
    chosen_row = jnp.any(named, axis=1)
    slot_of_row = jnp.cumsum(chosen_row.astype(jnp.int32)) - 1
    place = slot_of_row[:, None] == jnp.arange(CAP, dtype=jnp.int32)[None, :]
    place = (place & chosen_row[:, None]).astype(BF16)
    return place, jnp.sum(jnp.where(named, route_weight, 0.0), axis=1, keepdims=True)


def near_first(i):
    return i


def far_first(i):
    return ((i & 1) << 1) | (i >> 1)


def take_kernel(rows, order, place_ref, source, *targets):
    for t, target in enumerate(targets):
        core = place_ref[1] if t else 1 - place_ref[1]
        for i in range(4):
            block = 2 * (place_ref[0] ^ order(i)) + core
            start = pl.multiple_of(block * rows, rows)
            target[:, i * rows : (i + 1) * rows] = source[:, pl.ds(start, rows)]


def take_columns(array, rows, order, count, place):
    half = jax.ShapeDtypeStruct((array.shape[0], 4 * rows), array.dtype)
    return pl.pallas_call(
        functools.partial(take_kernel, rows, order),
        out_shape=(half,) * count,
        in_specs=[
            pl.BlockSpec(memory_space=pltpu.SMEM),
            pl.BlockSpec(memory_space=pltpu.VMEM),
        ],
        out_specs=(pl.BlockSpec(memory_space=pltpu.VMEM),) * count,
        cost_estimate=pl.CostEstimate(
            flops=0, bytes_accessed=count * array.size * 2, transcendentals=0
        ),
    )(place, array)


def product_kernel(place_ref, own, got, own_pre, got_pre, out):
    total = lax.dot_general(own[...], own_pre[...], BY_TOKENS, preferred_element_type=F32)
    total += lax.dot_general(got[...], got_pre[...], BY_TOKENS, preferred_element_type=F32)
    out[...] = total.astype(out.dtype)


def token_product(own, got, own_pre, got_pre, place, first, dtype):
    tokens, width = own_pre.shape
    rows = got.shape[1] // 4
    pre = pl.BlockSpec((tokens, width), lambda i, p: (0, 0))

    def own_block(i, p):
        return 0, 2 * (p[0] ^ far_first(first + i)) + p[1]

    return pl.pallas_call(
        product_kernel,
        out_shape=jax.ShapeDtypeStruct((2 * rows, width), dtype),
        grid_spec=pltpu.PrefetchScalarGridSpec(
            num_scalar_prefetch=1,
            grid=(2,),
            in_specs=[
                pl.BlockSpec((tokens, rows), own_block),
                pl.BlockSpec((tokens, rows), lambda i, p: (0, first + i)),
                pre,
                pre,
            ],
            out_specs=pl.BlockSpec((rows, width), lambda i, p: (i, 0)),
        ),
        compiler_params=pltpu.CompilerParams(vmem_limit_bytes=32 << 20),
        cost_estimate=pl.CostEstimate(
            flops=8 * tokens * rows * width,
            bytes_accessed=8 * tokens * (width + rows),
            transcendentals=0,
        ),
    )(place, own, got, own_pre, got_pre)


def spread_kernel(place_ref, slots, weight, values, out):
    rows = out.shape[1] // 8
    for i in range(8):
        unit = place_ref[0] ^ ((i >> 2) | ((i & 1) << 1))
        block = 2 * unit + (place_ref[1] ^ ((i >> 1) & 1))
        placed = jnp.dot(
            slots[...], values[:, i * rows : (i + 1) * rows], preferred_element_type=F32
        )
        start = pl.multiple_of(block * rows, rows)
        out[:, pl.ds(start, rows)] = (weight[...] * placed).astype(out.dtype)


def spread(values, slots, weight, place):
    count, width = slots.shape[0], values.shape[1]
    step = count // 4
    return pl.pallas_call(
        spread_kernel,
        out_shape=jax.ShapeDtypeStruct((count, width), BF16),
        grid_spec=pltpu.PrefetchScalarGridSpec(
            num_scalar_prefetch=1,
            grid=(4,),
            in_specs=[
                pl.BlockSpec((step, CAP), lambda i, p: (i, 0)),
                pl.BlockSpec((step, 1), lambda i, p: (i, 0)),
                pl.BlockSpec((CAP, width), lambda i, p: (0, 0)),
            ],
            out_specs=pl.BlockSpec((step, width), lambda i, p: (i, 0)),
        ),
        compiler_params=pltpu.CompilerParams(vmem_limit_bytes=32 << 20),
    )(place, slots, weight, values)


def on_line(
    learn_in,
    learn_cot,
    preact,
    hidden_cot,
    master,
    moment,
    second,
    rollout_in,
    routes,
    route_weight,
):
    index = lax.axis_index("fsdp")
    grp = lax.axis_index("grp")
    tp = lax.axis_index("tp")
    line = jnp.stack([index // 2, index % 2])
    rows = master.shape[1]
    width = preact.shape[2]
    cut = 2 * width // 3
    last = None

    def swap(block, pairs):
        return lax.ppermute(block, "fsdp", pairs)

    def step(array):
        nonlocal last
        if last is not None:
            array = lax.optimization_barrier((array, last))[0]
        last = array
        return array

    def given(own, got, pre, got_pre):
        return token_product(own, got, pre, got_pre, line, 2, BF16)

    def kept(own, got, pre, got_pre):
        return token_product(own, got, pre, got_pre, line, 0, F32)

    def pair_sum(own, other):
        total = own + other.astype(F32)
        return total[:rows], total[rows:].astype(BF16)

    def updated(which, span, own, other):
        return adam(
            master[0, :, which, span],
            moment[0, :, which, span],
            second[0, :, which, span],
            own + other.astype(F32),
        )

    hidden_act, grad_gate, grad_up = activations(preact, hidden_cot)
    (cot_give,) = take_columns(learn_cot, rows, far_first, 1, line)
    hidden_act = step(hidden_act)
    down_args = (learn_cot, swap(cot_give, CORES), hidden_act, swap(hidden_act, CORES))
    d_given = step(given(*down_args))
    d_got = swap(d_given, NEAR)

    place, weight = slots(routes, route_weight)
    picked = lax.dot_general(step(place), rollout_in, BY_TOKENS, preferred_element_type=F32)
    picked = step(picked.astype(BF16))
    row_give, row_keep = take_columns(picked, rows, near_first, 2, line)
    row_got = swap(step(row_give), CORES)
    (in_give,) = take_columns(step(learn_in), rows, far_first, 1, line)
    in_got = swap(step(in_give), CORES)
    grad_gate = step(grad_gate)
    gate_args = (learn_in, in_got, grad_gate, swap(grad_gate, CORES))
    here = step(jnp.stack([row_keep, row_got]))
    there = swap(here[..., 2 * rows :], FAR)
    g_given = step(given(*gate_args))
    d_kept = step(kept(*down_args))
    d_own, d_give = pair_sum(d_kept, d_got)
    d_give = step(d_give)
    d_across = swap(d_give, FAR)
    g_got = swap(step(g_given), NEAR)

    both = step(jnp.stack([here[..., : 2 * rows], there], axis=1))
    turned = lax.ppermute(both, ("grp", "tp"), TURN)
    other = lax.ppermute(both, ("grp", "tp"), ROUND)
    grad_up = step(grad_up)
    got_up = swap(grad_up, CORES)
    u_args = (learn_in, in_got, grad_up[:, :cut], got_up[:, :cut])
    v_args = (learn_in, in_got, grad_up[:, cut:], got_up[:, cut:])
    u_given = step(given(*u_args))
    g_kept = step(kept(*gate_args))
    whole = slice(None)
    d_all = updated(2, whole, d_own, d_across)
    d_shard = step(d_all[0].astype(BF16))
    d_other = swap(d_shard, FAR)
    g_own, g_give = pair_sum(g_kept, g_got)
    g_give = step(g_give)
    g_across = swap(g_give, FAR)
    u_got = swap(step(u_given), NEAR)

    mine = jnp.where(tp == grp, turned, other)
    theirs = jnp.where(tp == grp, other, turned)
    slot_rows = step(jnp.stack([mine, theirs], axis=1).reshape(-1, 2 * rows))
    v_given = step(given(*v_args))
    u_kept = step(kept(*u_args))
    v_kept = step(kept(*v_args))
    d_near = step(jnp.concatenate([d_shard, d_other]))
    vertical = lax.ppermute(d_near, "grp", SWAP)
    g_all = updated(0, whole, g_own, g_across)
    g_shard = step(g_all[0].astype(BF16))
    g_near = swap(g_shard, NEAR)
    u_own, u_give = pair_sum(u_kept, u_got)
    u_give = step(u_give)
    u_across = swap(u_give, FAR)
    v_got = swap(step(v_given), NEAR)

    diagonal = grp == tp
    first = jnp.where(diagonal, d_near, vertical)
    second_half = lax.ppermute(step(jnp.where(diagonal, vertical, d_near)), "tp", SWAP)

    def slot_product(shard, other):
        total = jnp.dot(slot_rows[:, :rows], shard, preferred_element_type=F32)
        return total + jnp.dot(slot_rows[:, rows:], other, preferred_element_type=F32)

    def fold(total, axis, pairs):
        keep, give = jnp.split(total, 2)
        return keep + lax.ppermute(step(give.astype(BF16)), axis, pairs).astype(F32)

    g_part = fold(slot_product(g_shard, g_near), "fsdp", CORES)
    u_all = updated(1, slice(0, cut), u_own, u_across)
    u_shard = step(u_all[0].astype(BF16))
    u_near = swap(u_shard, NEAR)
    v_own, v_give = pair_sum(v_kept, v_got)
    v_give = step(v_give)
    v_across = swap(v_give, FAR)
    g_part = fold(g_part, "grp", SWAP)
    v_all = updated(1, slice(cut, width), v_own, v_across)
    v_shard = step(v_all[0].astype(BF16))
    v_near = swap(v_shard, NEAR)
    gate_pre = fold(g_part, "fsdp", FAR)
    u_part = fold(slot_product(u_shard, u_near), "fsdp", CORES)
    u_part = fold(u_part, "grp", SWAP)
    v_part = fold(slot_product(v_shard, v_near), "fsdp", CORES)
    v_part = fold(v_part, "grp", SWAP)
    u_part = fold(u_part, "fsdp", FAR)
    v_part = fold(v_part, "fsdp", FAR)
    up_pre = jnp.concatenate([u_part, v_part], axis=1)
    down = jnp.concatenate([first, second_half], axis=1)
    down = jnp.concatenate([down, swap(down, CORES)])

    hidden = (jax.nn.silu(gate_pre) * up_pre).astype(BF16)
    near_hidden = swap(hidden, NEAR)
    hidden = jnp.concatenate([hidden, lax.ppermute(hidden, "tp", SWAP)], axis=1)
    near_hidden = jnp.concatenate([near_hidden, lax.ppermute(near_hidden, "tp", SWAP)], axis=1)
    near_out = lax.dot_general(near_hidden, down, BY_LAST, preferred_element_type=F32)
    near_out = swap(near_out.astype(BF16), NEAR)
    out = lax.dot_general(hidden, down, BY_LAST, preferred_element_type=F32).astype(BF16)
    slot_out = jnp.concatenate([out, near_out], axis=1)
    expert_out = spread(slot_out, place, weight, line)
    up_all = [jnp.concatenate([u_all[i], v_all[i]], axis=1) for i in range(3)]
    outs = [jnp.stack([g_all[i], up_all[i], d_all[i]], axis=1)[None] for i in range(3)]
    return (*outs, expert_out)


def on_device(
    learn_in,
    learn_cot,
    preact,
    hidden_cot,
    master,
    moment,
    second,
    rollout_in,
    routes,
    route_weight,
):
    hidden_width = preact.shape[2]
    hidden_act, grad_gate, grad_up = activations(preact, hidden_cot)
    pre_grads = jnp.concatenate([grad_gate, grad_up], axis=1)
    front = lax.dot_general(
        learn_in, pre_grads, BY_TOKENS, preferred_element_type=F32
    ).reshape(master.shape[1] * lax.axis_size("fsdp"), 2, hidden_width)
    back = lax.dot_general(learn_cot, hidden_act, BY_TOKENS, preferred_element_type=F32)[:, None, :]
    grad = lax.psum_scatter(
        jnp.concatenate([front, back], axis=1).astype(BF16),
        "fsdp",
        scatter_dimension=0,
        tiled=True,
    ).astype(F32)[None]
    master_new, moment_new, second_new = adam(master, moment, second, grad)
    half_rows = lax.all_gather(master_new.astype(BF16), "fsdp", axis=1, tiled=True)
    passed = lax.all_gather(half_rows, "grp", axis=0, tiled=True).reshape(-1, 3, hidden_width)
    weight_in = passed[:, :2, :].reshape(-1, 2 * hidden_width)
    place, weight = slots(routes, route_weight)
    picked = lax.dot_general(place, rollout_in, BY_TOKENS, preferred_element_type=F32).astype(BF16)
    slot_rows = lax.all_gather(picked, "tp", axis=1, tiled=True)
    slot_pre = jnp.dot(slot_rows, weight_in, preferred_element_type=F32)
    slot_hidden = jax.nn.silu(slot_pre[:, :hidden_width]) * slot_pre[:, hidden_width:]
    partial_out = lax.dot_general(
        slot_hidden.astype(BF16), passed[:, 2, :], BY_LAST, preferred_element_type=F32
    )
    slot_out = lax.psum_scatter(
        partial_out.astype(BF16), "tp", scatter_dimension=1, tiled=True
    )
    placed = jnp.dot(place, slot_out, preferred_element_type=F32)
    expert_out = (weight * placed).astype(BF16)
    return (master_new, moment_new, second_new, expert_out)


def solution(mesh):
    in_specs = (
        P("fsdp", "grp"),
        P("fsdp", "grp"),
        P("fsdp", None, "tp"),
        P("fsdp", "tp"),
        P("grp", "fsdp", None, "tp"),
        P("grp", "fsdp", None, "tp"),
        P("grp", "fsdp", None, "tp"),
        P(("fsdp", "grp"), "tp"),
        P(("fsdp", "grp"), None),
        P(("fsdp", "grp"), None),
    )
    out_specs = (
        P("grp", "fsdp", None, "tp"),
        P("grp", "fsdp", None, "tp"),
        P("grp", "fsdp", None, "tp"),
        P(("fsdp", "grp"), "tp"),
    )
    small = (mesh.shape["fsdp"], mesh.shape["grp"], mesh.shape["tp"]) == (8, 2, 2)
    return jax.shard_map(
        on_line if small else on_device,
        mesh=mesh,
        in_specs=in_specs,
        out_specs=out_specs,
        check_vma=False,
    )
```

profile of v0, /device:TPU:0, one launch (start us, length us, event | category | flops | bytes accessed | tf_op | source)
XLA Modules:
  0.0 191.3 jit_solution(321626416521054210)
XLA Ops:
  1.3 2.3 %shard_map.129 = bf16[344,1024]{1,0:T(8,128)(2,1)} custom-call(s32[2]{0:T(128)} %pad_add_fusion.place_ref, bf16[344,2048]{1,0:T(8,128)(2,1)} %own.11), custom_call_target="tpu_custom_call" | custom-call | bytes 1409024 | tf_op jit(solution)/shard_map/pallas_call | solution.py:81
  4.1 1.5 fusion.55
  5.7 1.8 fusion.8
  8.5 1.3 collective-permute-done.1.got_pre
  9.8 3.9 %shard_map.130 = bf16[512,768]{1,0:T(8,128)(2,1)} custom-call(s32[2]{0:T(128)S(1)} %copy-done.11, bf16[344,2048]{1,0:T(8,128)(2,1)S(1)} %copy-done.3, bf16[344,1024]{1,0:T(8,128)(2,1)} %collective-permute-done.got, bf16[344,768]{1,0:T(8,128)(2,1)} %get-tuple-element.107.own_pre, bf16[344,768]{1,0:T(8,128)(2,1)} %collective-permute-done.1.got_pre), custom_call_target="tpu_custom_call" | custom-call | flops 541065216 | bytes 2818048 | tf_op jit(solution)/shard_map/pallas_call | solution.py:109
  13.7 2.7 %collective-permute-start.6 = (bf16[512,768]{1,0:T(8,128)(2,1)}, bf16[512,768]{1,0:T(8,128)(2,1)}, u32[]{:S(2)}, u32[]{:S(2)}) collective-permute-start(bf16[512,768]{1,0:T(8,128)(2,1)} %shard_map.130), channel_id=1, source_target_pairs={{0,8},{4,12},{8,0},{12,4},{16,24},{20,28},{24,16},{28,20},{1,9},{5... | collective-permute-start | bytes 2359304 | tf_op jit(solution)/shard_map/ppermute | solution.py:186
  17.7 1.9 shard_map.131
  19.5 2.3 %shard_map.132 = bf16[344,1024]{1,0:T(8,128)(2,1)} custom-call(s32[2]{0:T(128)} %pad_add_fusion.place_ref, bf16[344,2048]{1,0:T(8,128)(2,1)} %own.15), custom_call_target="tpu_custom_call" | custom-call | bytes 1409024 | tf_op jit(solution)/shard_map/pallas_call | solution.py:81
  22.5 3.2 %shard_map.135 = f32[512,768]{1,0:T(8,128)S(1)} custom-call(s32[2]{0:T(128)S(1)} %copy-done.12, bf16[344,2048]{1,0:T(8,128)(2,1)S(1)} %copy-done.3, bf16[344,1024]{1,0:T(8,128)(2,1)} %collective-permute-done.got, bf16[344,768]{1,0:T(8,128)(2,1)} %get-tuple-element.107.own_pre, bf16[344,768]{1,0:T(8,128)(2,1)} %collective-permute-done.1.got_pre), custom_call_target="tpu_custom_call" | custom-call | flops 541065216 | bytes 2818048 | tf_op jit(solution)/shard_map/pallas_call | solution.py:109
  25.8 2.6 %collective-permute-start.5 = (bf16[2,112,512]{2,1,0:T(8,128)(2,1)S(1)}, bf16[2,112,512]{2,1,0:T(8,128)(2,1)S(1)}, u32[]{:S(2)}, u32[]{:S(2)}) collective-permute-start(bf16[2,112,512]{2,1,0:T(8,128)(2,1)S(1)} %get-tuple-element.116), channel_id=1, source_target_pairs={{0,16},{4,20},{8,24},{12,28},{16,0},{20,4},{24,8},{28,12},{1,17},{... | collective-permute-start | bytes 688136 | tf_op jit(solution)/shard_map/ppermute | solution.py:186
  28.4 2.7 %shard_map.134 = bf16[512,768]{1,0:T(8,128)(2,1)} custom-call(s32[2]{0:T(128)S(1)} %copy-done.12, bf16[344,2048]{1,0:T(8,128)(2,1)S(1)} %copy-done.2, bf16[344,1024]{1,0:T(8,128)(2,1)S(1)} %collective-permute-done.2.got, bf16[344,768]{1,0:T(8,128)(2,1)S(1)} %copy-done.4, bf16[344,768]{1,0:T(8,128)(2,1)S(1)} %collective-permute-done.3.got_pre), custom_call_target="tpu_custom_call" | custom-call | flops 541065216 | bytes 2818048 | tf_op jit(solution)/shard_map/pallas_call | solution.py:109
  31.1 8.6 %collective-permute-done.6 = bf16[512,768]{1,0:T(8,128)(2,1)} collective-permute-done((bf16[512,768]{1,0:T(8,128)(2,1)}, bf16[512,768]{1,0:T(8,128)(2,1)}, u32[]{:S(2)}, u32[]{:S(2)}) %collective-permute-start.6) | collective-permute-done | bytes 786464 | tf_op jit(solution)/shard_map/ppermute | solution.py:186
  39.7 1.3 convert_add_fusion.1
  42.3 1.9 collective-permute-start.9
  44.1 2.5 %collective-permute-start.8 = (bf16[512,768]{1,0:T(8,128)(2,1)}, bf16[512,768]{1,0:T(8,128)(2,1)}, u32[]{:S(2)}, u32[]{:S(2)}) collective-permute-start(bf16[512,768]{1,0:T(8,128)(2,1)} %shard_map.134), channel_id=1, source_target_pairs={{0,8},{4,12},{8,0},{12,4},{16,24},{20,28},{24,16},{28,20},{1,9},{5... | collective-permute-start | bytes 2359304 | tf_op jit(solution)/shard_map/ppermute | solution.py:186
  49.3 1.9 %shard_map.133 = f32[512,768]{1,0:T(8,128)S(1)} custom-call(s32[2]{0:T(128)S(1)} %copy-done.12, bf16[344,2048]{1,0:T(8,128)(2,1)S(1)} %copy-done.2, bf16[344,1024]{1,0:T(8,128)(2,1)S(1)} %collective-permute-done.2.got, bf16[344,768]{1,0:T(8,128)(2,1)S(1)} %copy-done.5, bf16[344,768]{1,0:T(8,128)(2,1)S(1)} %copy-done.7), custom_call_target="tpu_custom_call" | custom-call | flops 541065216 | bytes 2818048 | tf_op jit(solution)/shard_map/pallas_call | solution.py:109
  53.0 4.4 %collective-permute-start.12 = (bf16[2,2,112,512]{3,2,0,1:T(8,128)(2,1)S(1)}, bf16[2,2,112,512]{3,2,0,1:T(8,128)(2,1)S(1)}, u32[]{:S(2)}, u32[]{:S(2)}) collective-permute-start(bf16[2,2,112,512]{3,2,0,1:T(8,128)(2,1)S(1)} %copy-done.20), channel_id=1, source_target_pairs={{0,1},{1,3},{3,2},{2,0},{4,5},{5,7},{7,6},{6,4},{8,9},{9,11},{11,1... | collective-permute-start | bytes 1376264 | tf_op jit(solution)/shard_map/ppermute | solution.py:240
  58.4 4.5 %collective-permute-done.9 = bf16[256,768]{1,0:T(8,128)(2,1)} collective-permute-done((bf16[256,768]{1,0:T(8,128)(2,1)}, bf16[256,768]{1,0:T(8,128)(2,1)}, u32[]{:S(2)}, u32[]{:S(2)}) %collective-permute-start.9) | collective-permute-done | bytes 393248 | tf_op jit(solution)/shard_map/ppermute | solution.py:186
  62.8 2.2 %fusion.54 = (bf16[256,768]{1,0:T(8,128)(2,1)S(1)}, f32[256,768]{1,0:T(8,128)S(1)}, f32[256,1,768]{2,0,1:T(8,128)S(1)}, f32[256,1,768]{2,0,1:T(8,128)S(1)}) fusion(f32[1,256,3,768]{3,1,2,0:T(8,128)S(1)} %copy-done.16, bf16[256,768]{1,0:T(8,128)(2,1)} %collective-permute-done.9, f32[512,768]{1,0:T(8,128)S(1)} %copy-done.14, f32[1,256,3,768]{3,1,2,0:T(8,128)} %param.15, ...), kind=kLoop, calls=%fused_computation.136 | loop fusion | flops 3538944 | bytes 6291456 | tf_op jit(solution)/shard_map/convert_element_type | solution.py:249
  66.0 1.6 shard_map.136
  67.8 5.4 %collective-permute-done.8 = bf16[512,768]{1,0:T(8,128)(2,1)} collective-permute-done((bf16[512,768]{1,0:T(8,128)(2,1)}, bf16[512,768]{1,0:T(8,128)(2,1)}, u32[]{:S(2)}, u32[]{:S(2)}) %collective-permute-start.8) | collective-permute-done | bytes 786464 | tf_op jit(solution)/shard_map/ppermute | solution.py:186
  76.1 1.4 shard_map.138
  77.5 1.4 shard_map.139
  78.9 1.6 shard_map.137
  81.5 15.6 %collective-permute-done.14 = bf16[256,768]{1,0:T(8,128)(2,1)S(1)} collective-permute-done((bf16[256,768]{1,0:T(8,128)(2,1)S(1)}, bf16[256,768]{1,0:T(8,128)(2,1)S(1)}, u32[]{:S(2)}, u32[]{:S(2)}) %collective-permute-start.14) | collective-permute-done | bytes 393248 | tf_op jit(solution)/shard_map/ppermute | solution.py:186
  97.2 1.6 collective-permute-start.18
  98.7 5.4 %collective-permute-done.10 = bf16[256,768]{1,0:T(8,128)(2,1)S(1)} collective-permute-done((bf16[256,768]{1,0:T(8,128)(2,1)S(1)}, bf16[256,768]{1,0:T(8,128)(2,1)S(1)}, u32[]{:S(2)}, u32[]{:S(2)}) %collective-permute-start.10) | collective-permute-done | bytes 393248 | tf_op jit(solution)/shard_map/ppermute | solution.py:186
  105.4 3.3 %collective-permute-done.13 = bf16[512,512]{1,0:T(8,128)(2,1)S(1)} collective-permute-done((bf16[512,512]{1,0:T(8,128)(2,1)S(1)}, bf16[512,512]{1,0:T(8,128)(2,1)S(1)}, u32[]{:S(2)}, u32[]{:S(2)}) %collective-permute-start.13) | collective-permute-done | bytes 524320 | tf_op jit(solution)/shard_map/ppermute | solution.py:186
  109.0 1.5 collective-permute-start.16
  110.5 12.2 %collective-permute-done.17 = bf16[256,768]{1,0:T(8,128)(2,1)S(1)} collective-permute-done((bf16[256,768]{1,0:T(8,128)(2,1)S(1)}, bf16[256,768]{1,0:T(8,128)(2,1)S(1)}, u32[]{:S(2)}, u32[]{:S(2)}) %collective-permute-start.17) | collective-permute-done | bytes 393248 | tf_op jit(solution)/shard_map/ppermute | solution.py:186
  123.4 3.7 %collective-permute-done.16 = bf16[512,256]{1,0:T(8,128)(2,1)S(1)} collective-permute-done((bf16[512,256]{1,0:T(8,128)(2,1)S(1)}, bf16[512,256]{1,0:T(8,128)(2,1)S(1)}, u32[]{:S(2)}, u32[]{:S(2)}) %collective-permute-start.16) | collective-permute-done | bytes 262176 | tf_op jit(solution)/shard_map/ppermute | solution.py:186
  129.3 1.9 collective-permute-start.23
  131.2 1.5 collective-permute-start.32
  132.7 4.5 %collective-permute-done.19 = bf16[256,256]{1,0:T(8,128)(2,1)S(1)} collective-permute-done((bf16[256,256]{1,0:T(8,128)(2,1)S(1)}, bf16[256,256]{1,0:T(8,128)(2,1)S(1)}, u32[]{:S(2)}, u32[]{:S(2)}) %collective-permute-start.19) | collective-permute-done | bytes 131104 | tf_op jit(solution)/shard_map/ppermute | solution.py:186
  137.7 1.6 collective-permute-start.21
  141.1 6.6 %collective-permute-done.21 = bf16[224,768]{1,0:T(8,128)(2,1)S(1)} collective-permute-done((bf16[224,768]{1,0:T(8,128)(2,1)S(1)}, bf16[224,768]{1,0:T(8,128)(2,1)S(1)}, u32[]{:S(2)}, u32[]{:S(2)}) %collective-permute-start.21) | collective-permute-done | bytes 344096 | tf_op jit(solution)/shard_map/ppermute | solution.py:282
  151.2 1.5 collective-permute-start.25
  153.4 6.3 %collective-permute-done.25 = bf16[224,512]{1,0:T(8,128)(2,1)S(1)} collective-permute-done((bf16[224,512]{1,0:T(8,128)(2,1)S(1)}, bf16[224,512]{1,0:T(8,128)(2,1)S(1)}, u32[]{:S(2)}, u32[]{:S(2)}) %collective-permute-start.25) | collective-permute-done | bytes 229408 | tf_op jit(solution)/shard_map/ppermute | solution.py:282
  159.8 2.5 %collective-permute-start.28 = (bf16[112,512]{1,0:T(8,128)(2,1)S(1)}, bf16[112,512]{1,0:T(8,128)(2,1)S(1)}, u32[]{:S(2)}, u32[]{:S(2)}) collective-permute-start(bf16[112,512]{1,0:T(8,128)(2,1)S(1)} %split.126), channel_id=1, source_target_pairs={{0,16},{4,20},{8,24},{12,28},{16,0},{20,4},{24,8},{28,12},{1,17},{... | collective-permute-start | bytes 344072 | tf_op jit(solution)/shard_map/ppermute | solution.py:282
  162.3 1.6 collective-permute-start.30
  163.9 4.7 %collective-permute-done.28 = bf16[112,512]{1,0:T(8,128)(2,1)S(1)} collective-permute-done((bf16[112,512]{1,0:T(8,128)(2,1)S(1)}, bf16[112,512]{1,0:T(8,128)(2,1)S(1)}, u32[]{:S(2)}, u32[]{:S(2)}) %collective-permute-start.28) | collective-permute-done | bytes 114720 | tf_op jit(solution)/shard_map/ppermute | solution.py:282
  169.5 2.6 %maximum_bitcast_fusion.1 = (f32[1,256,3,768]{3,1,2,0:T(8,128)}, f32[1,256,3,768]{3,1,2,0:T(8,128)}) fusion(f32[256,1,768]{2,0,1:T(8,128)S(1)} %get-tuple-element.105, f32[256,1,768]{2,0,1:T(8,128)S(1)} %maximum_bitcast_fusion.4, f32[256,1,768]{2,0,1:T(8,128)S(1)} %get-tuple-element.103, f32[256,1,768]{2,0,1:T(8,128)S(1)} %get-tuple-element.104, ...), kind=kLoop, calls=%fused_computation.3 | loop fusion | flops 2359296 | bytes 9437184 | tf_op jit(solution)/shard_map/broadcast_in_dim | solution.py:316
  172.1 2.8 %collective-permute-done.34 = bf16[112,768]{1,0:T(8,128)(2,1)S(1)} collective-permute-done((bf16[112,768]{1,0:T(8,128)(2,1)S(1)}, bf16[112,768]{1,0:T(8,128)(2,1)S(1)}, u32[]{:S(2)}, u32[]{:S(2)}) %collective-permute-start.34) | collective-permute-done | bytes 172064 | tf_op jit(solution)/shard_map/ppermute | solution.py:186
  174.9 1.5 collective-permute-start.35
  176.4 1.6 maximum_bitcast_fusion
  178.5 2.5 %collective-permute-done.35 = bf16[112,768]{1,0:T(8,128)(2,1)S(1)} collective-permute-done((bf16[112,768]{1,0:T(8,128)(2,1)S(1)}, bf16[112,768]{1,0:T(8,128)(2,1)S(1)}, u32[]{:S(2)}, u32[]{:S(2)}) %collective-permute-start.35) | collective-permute-done | bytes 172064 | tf_op jit(solution)/shard_map/ppermute | solution.py:309
  184.4 3.8 %collective-permute-done.36 = bf16[112,1024]{1,0:T(8,128)(2,1)S(1)} collective-permute-done((bf16[112,1024]{1,0:T(8,128)(2,1)S(1)}, bf16[112,1024]{1,0:T(8,128)(2,1)S(1)}, u32[]{:S(2)}, u32[]{:S(2)}) %collective-permute-start.36) | collective-permute-done | bytes 229408 | tf_op jit(solution)/shard_map/ppermute | solution.py:186
  188.3 3.1 %shard_map.140 = bf16[512,2048]{1,0:T(8,128)(2,1)} custom-call(s32[2]{0:T(128)S(1)} %copy-done.12, bf16[512,112]{1,0:T(8,128)(2,1)S(1)} %copy-done.9, f32[512,1]{1,0:T(8,128)S(1)} %copy-done.10, bf16[112,2048]{1,0:T(8,128)(2,1)S(1)} %pad_maximum_fusion.12.values), custom_call_target="tpu_custom_call" | custom-call | tf_op jit(solution)/shard_map/pallas_call | solution.py:147
  (157 shorter events, 31.3 us)
Async XLA Ops:
  0.6 15.8 %copy-start = (bf16[512,2048]{1,0:T(8,128)(2,1)S(1)}, bf16[512,2048]{1,0:T(8,128)(2,1)}, u32[]{:S(2)}) copy-start(bf16[512,2048]{1,0:T(8,128)(2,1)} %param.17) | copy-start | bytes 6291460
  3.7 6.1 %collective-permute-start = (bf16[344,1024]{1,0:T(8,128)(2,1)}, bf16[344,1024]{1,0:T(8,128)(2,1)}, u32[]{:S(2)}, u32[]{:S(2)}) collective-permute-start(bf16[344,1024]{1,0:T(8,128)(2,1)} %shard_map.129), channel_id=1, source_target_pairs={{0,4},{4,0},{8,12},{12,8},{16,20},{20,16},{24,28},{28,24},{1,5},{5... | collective-permute-start | bytes 2113544 | tf_op jit(solution)/shard_map/ppermute | solution.py:186
  7.5 2.3 %collective-permute-start.1 = (bf16[344,768]{1,0:T(8,128)(2,1)}, bf16[344,768]{1,0:T(8,128)(2,1)}, u32[]{:S(2)}, u32[]{:S(2)}) collective-permute-start(bf16[344,768]{1,0:T(8,128)(2,1)} %get-tuple-element.107.own_pre), channel_id=1, source_target_pairs={{0,4},{4,0},{8,12},{12,8},{16,20},{20,16},{24,28},{28,24},{1,5},{5... | collective-permute-start | bytes 1585160 | tf_op jit(solution)/shard_map/ppermute | solution.py:186
  8.4 7.9 %copy-start.8 = (bf16[512,112]{1,0:T(8,128)(2,1)}, bf16[512,112]{1,0:T(8,128)(2,1)S(1)}, u32[]{:S(2)}) copy-start(bf16[512,112]{1,0:T(8,128)(2,1)S(1)} %fusion.42.slots) | copy-start | bytes 344068
  13.7 8.8 %copy-start.12 = (s32[2]{0:T(128)S(1)}, s32[2]{0:T(128)}, u32[]{:S(2)}) copy-start(s32[2]{0:T(128)} %pad_add_fusion.place_ref) | copy-start | bytes 28
  13.7 26.0 %collective-permute-start.6 = (bf16[512,768]{1,0:T(8,128)(2,1)}, bf16[512,768]{1,0:T(8,128)(2,1)}, u32[]{:S(2)}, u32[]{:S(2)}) collective-permute-start(bf16[512,768]{1,0:T(8,128)(2,1)} %shard_map.130), channel_id=1, source_target_pairs={{0,8},{4,12},{8,0},{12,4},{16,24},{20,28},{24,16},{28,20},{1,9},{5... | collective-permute-start | bytes 2359304 | tf_op jit(solution)/shard_map/ppermute | solution.py:186
  21.9 6.6 %collective-permute-start.2 = (bf16[344,1024]{1,0:T(8,128)(2,1)}, bf16[344,1024]{1,0:T(8,128)(2,1)S(1)}, u32[]{:S(2)}, u32[]{:S(2)}) collective-permute-start(bf16[344,1024]{1,0:T(8,128)(2,1)} %shard_map.132), channel_id=1, source_target_pairs={{0,4},{4,0},{8,12},{12,8},{16,20},{20,16},{24,28},{28,24},{1,5},{5... | collective-permute-start | bytes 2113544 | tf_op jit(solution)/shard_map/ppermute | solution.py:186
  22.0 3.7 %collective-permute-start.4 = (bf16[112,1024]{1,0:T(8,128)(2,1)}, bf16[112,1024]{1,0:T(8,128)(2,1)S(1)}, u32[]{:S(2)}, u32[]{:S(2)}) collective-permute-start(bf16[112,1024]{1,0:T(8,128)(2,1)} %get-tuple-element.50), channel_id=1, source_target_pairs={{0,4},{4,0},{8,12},{12,8},{16,20},{20,16},{24,28},{28,24},{1,5},{5... | collective-permute-start | bytes 688136 | tf_op jit(solution)/shard_map/ppermute | solution.py:186
  22.4 6.0 %collective-permute-start.3 = (bf16[344,768]{1,0:T(8,128)(2,1)}, bf16[344,768]{1,0:T(8,128)(2,1)S(1)}, u32[]{:S(2)}, u32[]{:S(2)}) collective-permute-start(bf16[344,768]{1,0:T(8,128)(2,1)} %get-tuple-element.53.own_pre), channel_id=1, source_target_pairs={{0,4},{4,0},{8,12},{12,8},{16,20},{20,16},{24,28},{28,24},{1,5},{5... | collective-permute-start | bytes 1585160 | tf_op jit(solution)/shard_map/ppermute | solution.py:186
  25.8 20.8 %collective-permute-start.5 = (bf16[2,112,512]{2,1,0:T(8,128)(2,1)S(1)}, bf16[2,112,512]{2,1,0:T(8,128)(2,1)S(1)}, u32[]{:S(2)}, u32[]{:S(2)}) collective-permute-start(bf16[2,112,512]{2,1,0:T(8,128)(2,1)S(1)} %get-tuple-element.116), channel_id=1, source_target_pairs={{0,16},{4,20},{8,24},{12,28},{16,0},{20,4},{24,8},{28,12},{1,17},{... | collective-permute-start | bytes 688136 | tf_op jit(solution)/shard_map/ppermute | solution.py:186
  28.4 12.6 %copy-start.6 = (bf16[344,768]{1,0:T(8,128)(2,1)}, bf16[344,768]{1,0:T(8,128)(2,1)S(1)}, u32[]{:S(2)}) copy-start(bf16[344,768]{1,0:T(8,128)(2,1)S(1)} %collective-permute-done.3.got_pre) | copy-start | bytes 1585156
  31.1 17.1 %copy-start.5 = (bf16[344,768]{1,0:T(8,128)(2,1)S(1)}, bf16[344,768]{1,0:T(8,128)(2,1)}, u32[]{:S(2)}) copy-start(bf16[344,768]{1,0:T(8,128)(2,1)} %get-tuple-element.53.own_pre) | copy-start | bytes 1585156
  42.3 20.6 %collective-permute-start.9 = (bf16[256,768]{1,0:T(8,128)(2,1)}, bf16[256,768]{1,0:T(8,128)(2,1)}, u32[]{:S(2)}, u32[]{:S(2)}) collective-permute-start(bf16[256,768]{1,0:T(8,128)(2,1)} %slice.230), channel_id=1, source_target_pairs={{0,16},{4,20},{8,24},{12,28},{16,0},{20,4},{24,8},{28,12},{1,17},{... | collective-permute-start | bytes 1179656 | tf_op jit(solution)/shard_map/ppermute | solution.py:186
  44.1 29.0 %collective-permute-start.8 = (bf16[512,768]{1,0:T(8,128)(2,1)}, bf16[512,768]{1,0:T(8,128)(2,1)}, u32[]{:S(2)}, u32[]{:S(2)}) collective-permute-start(bf16[512,768]{1,0:T(8,128)(2,1)} %shard_map.134), channel_id=1, source_target_pairs={{0,8},{4,12},{8,0},{12,4},{16,24},{20,28},{24,16},{28,20},{1,9},{5... | collective-permute-start | bytes 2359304 | tf_op jit(solution)/shard_map/ppermute | solution.py:186
  47.4 17.6 %collective-permute-start.7 = (bf16[344,768]{1,0:T(8,128)(2,1)}, bf16[344,768]{1,0:T(8,128)(2,1)}, u32[]{:S(2)}, u32[]{:S(2)}) collective-permute-start(bf16[344,768]{1,0:T(8,128)(2,1)} %get-tuple-element.61), channel_id=1, source_target_pairs={{0,4},{4,0},{8,12},{12,8},{16,20},{20,16},{24,28},{28,24},{1,5},{5... | collective-permute-start | bytes 1585160 | tf_op jit(solution)/shard_map/ppermute | solution.py:186
  49.3 13.5 %copy-start.14 = (f32[512,768]{1,0:T(8,128)S(1)}, f32[512,768]{1,0:T(8,128)}, u32[]{:S(2)}) copy-start(f32[512,768]{1,0:T(8,128)} %copy-done.13) | copy-start | bytes 4718596
  49.3 13.5 %copy-start.16 = (f32[1,256,3,768]{3,1,2,0:T(8,128)S(1)}, f32[1,256,3,768]{3,1,2,0:T(8,128)}, u32[]{:S(2)}) copy-start(f32[1,256,3,768]{3,1,2,0:T(8,128)} %param.16) | copy-start | bytes 7077892
  52.3 22.6 %collective-permute-start.11 = (bf16[2,2,112,512]{3,2,0,1:T(8,128)(2,1)S(1)}, bf16[2,2,112,512]{3,2,0,1:T(8,128)(2,1)S(1)}, u32[]{:S(2)}, u32[]{:S(2)}) collective-permute-start(bf16[2,2,112,512]{3,2,0,1:T(8,128)(2,1)S(1)} %copy-done.20), channel_id=1, source_target_pairs={{0,0},{1,2},{2,1},{3,3},{4,4},{5,6},{6,5},{7,7},{8,8},{9,10},{10,9... | collective-permute-start | bytes 1376264 | tf_op jit(solution)/shard_map/ppermute | solution.py:239
  53.0 21.9 %collective-permute-start.12 = (bf16[2,2,112,512]{3,2,0,1:T(8,128)(2,1)S(1)}, bf16[2,2,112,512]{3,2,0,1:T(8,128)(2,1)S(1)}, u32[]{:S(2)}, u32[]{:S(2)}) collective-permute-start(bf16[2,2,112,512]{3,2,0,1:T(8,128)(2,1)S(1)} %copy-done.20), channel_id=1, source_target_pairs={{0,1},{1,3},{3,2},{2,0},{4,5},{5,7},{7,6},{6,4},{8,9},{9,11},{11,1... | collective-permute-start | bytes 1376264 | tf_op jit(solution)/shard_map/ppermute | solution.py:240
  67.7 29.4 %collective-permute-start.14 = (bf16[256,768]{1,0:T(8,128)(2,1)S(1)}, bf16[256,768]{1,0:T(8,128)(2,1)S(1)}, u32[]{:S(2)}, u32[]{:S(2)}) collective-permute-start(bf16[256,768]{1,0:T(8,128)(2,1)S(1)} %get-tuple-element.64), channel_id=1, source_target_pairs={{0,16},{4,20},{8,24},{12,28},{16,0},{20,4},{24,8},{28,12},{1,17},{... | collective-permute-start | bytes 1179656 | tf_op jit(solution)/shard_map/ppermute | solution.py:186
  74.5 29.6 %collective-permute-start.10 = (bf16[256,768]{1,0:T(8,128)(2,1)S(1)}, bf16[256,768]{1,0:T(8,128)(2,1)S(1)}, u32[]{:S(2)}, u32[]{:S(2)}) collective-permute-start(bf16[256,768]{1,0:T(8,128)(2,1)S(1)} %slice.229), channel_id=1, source_target_pairs={{0,16},{4,20},{8,24},{12,28},{16,0},{20,4},{24,8},{28,12},{1,17},{... | collective-permute-start | bytes 1179656 | tf_op jit(solution)/shard_map/ppermute | solution.py:186
  78.9 25.2 %copy-start.17 = (f32[1,256,3,768]{3,1,2,0:T(8,128)S(1)}, f32[1,256,3,768]{3,1,2,0:T(8,128)}, u32[]{:S(2)}) copy-start(f32[1,256,3,768]{3,1,2,0:T(8,128)} %param.15) | copy-start | bytes 7077892
  78.9 25.2 %copy-start.18 = (f32[1,256,3,768]{3,1,2,0:T(8,128)S(1)}, f32[1,256,3,768]{3,1,2,0:T(8,128)}, u32[]{:S(2)}) copy-start(f32[1,256,3,768]{3,1,2,0:T(8,128)} %param.14) | copy-start | bytes 7077892
  80.6 28.1 %collective-permute-start.13 = (bf16[512,512]{1,0:T(8,128)(2,1)S(1)}, bf16[512,512]{1,0:T(8,128)(2,1)S(1)}, u32[]{:S(2)}, u32[]{:S(2)}) collective-permute-start(bf16[512,512]{1,0:T(8,128)(2,1)S(1)} %shard_map.136), channel_id=1, source_target_pairs={{0,8},{4,12},{8,0},{12,4},{16,24},{20,28},{24,16},{28,20},{1,9},{5... | collective-permute-start | bytes 1572872 | tf_op jit(solution)/shard_map/ppermute | solution.py:186
  97.2 30.4 %collective-permute-start.18 = (bf16[512,768]{1,0:T(8,128)(2,1)S(1)}, bf16[512,768]{1,0:T(8,128)(2,1)S(1)}, u32[]{:S(2)}, u32[]{:S(2)}) collective-permute-start(bf16[512,768]{1,0:T(8,128)(2,1)S(1)} %pad_maximum_fusion.9), channel_id=1, source_target_pairs={{0,2},{2,0},{1,3},{3,1},{4,6},{6,4},{5,7},{7,5},{8,10},{10,8},{9,1... | collective-permute-start | bytes 2359304 | tf_op jit(solution)/shard_map/ppermute | solution.py:263
  104.8 18.0 %collective-permute-start.17 = (bf16[256,768]{1,0:T(8,128)(2,1)S(1)}, bf16[256,768]{1,0:T(8,128)(2,1)S(1)}, u32[]{:S(2)}, u32[]{:S(2)}) collective-permute-start(bf16[256,768]{1,0:T(8,128)(2,1)S(1)} %get-tuple-element.72), channel_id=1, source_target_pairs={{0,8},{4,12},{8,0},{12,4},{16,24},{20,28},{24,16},{28,20},{1,9},{5... | collective-permute-start | bytes 1179656 | tf_op jit(solution)/shard_map/ppermute | solution.py:186
  108.9 18.2 %collective-permute-start.15 = (bf16[256,512]{1,0:T(8,128)(2,1)S(1)}, bf16[256,512]{1,0:T(8,128)(2,1)S(1)}, u32[]{:S(2)}, u32[]{:S(2)}) collective-permute-start(bf16[256,512]{1,0:T(8,128)(2,1)S(1)} %slice.231), channel_id=1, source_target_pairs={{0,16},{4,20},{8,24},{12,28},{16,0},{20,4},{24,8},{28,12},{1,17},{... | collective-permute-start | bytes 786440 | tf_op jit(solution)/shard_map/ppermute | solution.py:186
  109.0 18.1 %collective-permute-start.16 = (bf16[512,256]{1,0:T(8,128)(2,1)S(1)}, bf16[512,256]{1,0:T(8,128)(2,1)S(1)}, u32[]{:S(2)}, u32[]{:S(2)}) collective-permute-start(bf16[512,256]{1,0:T(8,128)(2,1)S(1)} %shard_map.138), channel_id=1, source_target_pairs={{0,8},{4,12},{8,0},{12,4},{16,24},{20,28},{24,16},{28,20},{1,9},{5... | collective-permute-start | bytes 786440 | tf_op jit(solution)/shard_map/ppermute | solution.py:186
  127.7 9.7 %collective-permute-start.20 = (bf16[448,768]{1,0:T(8,128)(2,1)S(1)}, bf16[448,768]{1,0:T(8,128)(2,1)S(1)}, u32[]{:S(2)}, u32[]{:S(2)}) collective-permute-start(bf16[448,768]{1,0:T(8,128)(2,1)S(1)} %split.119), channel_id=1, source_target_pairs={{0,4},{4,0},{8,12},{12,8},{16,20},{20,16},{24,28},{28,24},{1,5},{5... | collective-permute-start | bytes 2064392 | tf_op jit(solution)/shard_map/ppermute | solution.py:282
  127.8 9.3 %collective-permute-start.19 = (bf16[256,256]{1,0:T(8,128)(2,1)S(1)}, bf16[256,256]{1,0:T(8,128)(2,1)S(1)}, u32[]{:S(2)}, u32[]{:S(2)}) collective-permute-start(bf16[256,256]{1,0:T(8,128)(2,1)S(1)} %slice.232), channel_id=1, source_target_pairs={{0,16},{4,20},{8,24},{12,28},{16,0},{20,4},{24,8},{28,12},{1,17},{... | collective-permute-start | bytes 393224 | tf_op jit(solution)/shard_map/ppermute | solution.py:186
  129.3 11.3 %collective-permute-start.23 = (bf16[256,512]{1,0:T(8,128)(2,1)S(1)}, bf16[256,512]{1,0:T(8,128)(2,1)S(1)}, u32[]{:S(2)}, u32[]{:S(2)}) collective-permute-start(bf16[256,512]{1,0:T(8,128)(2,1)S(1)} %get-tuple-element.77), channel_id=1, source_target_pairs={{0,8},{4,12},{8,0},{12,4},{16,24},{20,28},{24,16},{28,20},{1,9},{5... | collective-permute-start | bytes 786440 | tf_op jit(solution)/shard_map/ppermute | solution.py:186
  131.2 19.3 %collective-permute-start.32 = (bf16[512,768]{1,0:T(8,128)(2,1)S(1)}, bf16[512,768]{1,0:T(8,128)(2,1)S(1)}, u32[]{:S(2)}, u32[]{:S(2)}) collective-permute-start(bf16[512,768]{1,0:T(8,128)(2,1)S(1)} %get-tuple-element.75), channel_id=1, source_target_pairs={{0,1},{1,0},{2,3},{3,2},{4,5},{5,4},{6,7},{7,6},{8,9},{9,8},{10,11... | collective-permute-start | bytes 2359304 | tf_op jit(solution)/shard_map/ppermute | solution.py:274
  137.7 10.0 %collective-permute-start.21 = (bf16[224,768]{1,0:T(8,128)(2,1)S(1)}, bf16[224,768]{1,0:T(8,128)(2,1)S(1)}, u32[]{:S(2)}, u32[]{:S(2)}) collective-permute-start(bf16[224,768]{1,0:T(8,128)(2,1)S(1)} %split.121), channel_id=1, source_target_pairs={{0,2},{2,0},{1,3},{3,1},{4,6},{6,4},{5,7},{7,5},{8,10},{10,8},{9,1... | collective-permute-start | bytes 1032200 | tf_op jit(solution)/shard_map/ppermute | solution.py:282
  141.1 7.1 %collective-permute-start.26 = (bf16[256,256]{1,0:T(8,128)(2,1)S(1)}, bf16[256,256]{1,0:T(8,128)(2,1)S(1)}, u32[]{:S(2)}, u32[]{:S(2)}) collective-permute-start(bf16[256,256]{1,0:T(8,128)(2,1)S(1)} %get-tuple-element.80), channel_id=1, source_target_pairs={{0,8},{4,12},{8,0},{12,4},{16,24},{20,28},{24,16},{28,20},{1,9},{5... | collective-permute-start | bytes 393224 | tf_op jit(solution)/shard_map/ppermute | solution.py:186
  147.8 1.9 collective-permute-start.24
  149.9 2.9 %collective-permute-start.27 = (bf16[448,256]{1,0:T(8,128)(2,1)S(1)}, bf16[448,256]{1,0:T(8,128)(2,1)S(1)}, u32[]{:S(2)}, u32[]{:S(2)}) collective-permute-start(bf16[448,256]{1,0:T(8,128)(2,1)S(1)} %split.122), channel_id=1, source_target_pairs={{0,4},{4,0},{8,12},{12,8},{16,20},{20,16},{24,28},{28,24},{1,5},{5... | collective-permute-start | bytes 688136 | tf_op jit(solution)/shard_map/ppermute | solution.py:282
  150.6 30.4 %collective-permute-start.33 = (bf16[512,1536]{1,0:T(8,128)(2,1)S(1)}, bf16[512,1536]{1,0:T(8,128)(2,1)S(1)}, u32[]{:S(2)}, u32[]{:S(2)}) collective-permute-start(bf16[512,1536]{1,0:T(8,128)(2,1)S(1)} %pad_maximum_fusion.1), channel_id=1, source_target_pairs={{0,4},{4,0},{8,12},{12,8},{16,20},{20,16},{24,28},{28,24},{1,5},{5... | collective-permute-start | bytes 4718600 | tf_op jit(solution)/shard_map/ppermute | solution.py:186
  150.7 18.6 %collective-permute-start.22 = (bf16[112,768]{1,0:T(8,128)(2,1)S(1)}, bf16[112,768]{1,0:T(8,128)(2,1)S(1)}, u32[]{:S(2)}, u32[]{:S(2)}) collective-permute-start(bf16[112,768]{1,0:T(8,128)(2,1)S(1)} %split.124), channel_id=1, source_target_pairs={{0,16},{4,20},{8,24},{12,28},{16,0},{20,4},{24,8},{28,12},{1,17},{... | collective-permute-start | bytes 516104 | tf_op jit(solution)/shard_map/ppermute | solution.py:282
  151.2 8.4 %collective-permute-start.25 = (bf16[224,512]{1,0:T(8,128)(2,1)S(1)}, bf16[224,512]{1,0:T(8,128)(2,1)S(1)}, u32[]{:S(2)}, u32[]{:S(2)}) collective-permute-start(bf16[224,512]{1,0:T(8,128)(2,1)S(1)} %split.123), channel_id=1, source_target_pairs={{0,2},{2,0},{1,3},{3,1},{4,6},{6,4},{5,7},{7,5},{8,10},{10,8},{9,1... | collective-permute-start | bytes 688136 | tf_op jit(solution)/shard_map/ppermute | solution.py:282
  152.8 9.5 %collective-permute-start.29 = (bf16[224,256]{1,0:T(8,128)(2,1)S(1)}, bf16[224,256]{1,0:T(8,128)(2,1)S(1)}, u32[]{:S(2)}, u32[]{:S(2)}) collective-permute-start(bf16[224,256]{1,0:T(8,128)(2,1)S(1)} %split.125), channel_id=1, source_target_pairs={{0,2},{2,0},{1,3},{3,1},{4,6},{6,4},{5,7},{7,5},{8,10},{10,8},{9,1... | collective-permute-start | bytes 344072 | tf_op jit(solution)/shard_map/ppermute | solution.py:282
  159.8 8.9 %collective-permute-start.28 = (bf16[112,512]{1,0:T(8,128)(2,1)S(1)}, bf16[112,512]{1,0:T(8,128)(2,1)S(1)}, u32[]{:S(2)}, u32[]{:S(2)}) collective-permute-start(bf16[112,512]{1,0:T(8,128)(2,1)S(1)} %split.126), channel_id=1, source_target_pairs={{0,16},{4,20},{8,24},{12,28},{16,0},{20,4},{24,8},{28,12},{1,17},{... | collective-permute-start | bytes 344072 | tf_op jit(solution)/shard_map/ppermute | solution.py:282
  162.3 6.9 %collective-permute-start.30 = (bf16[112,256]{1,0:T(8,128)(2,1)S(1)}, bf16[112,256]{1,0:T(8,128)(2,1)S(1)}, u32[]{:S(2)}, u32[]{:S(2)}) collective-permute-start(bf16[112,256]{1,0:T(8,128)(2,1)S(1)} %split.127), channel_id=1, source_target_pairs={{0,16},{4,20},{8,24},{12,28},{16,0},{20,4},{24,8},{28,12},{1,17},{... | collective-permute-start | bytes 172040 | tf_op jit(solution)/shard_map/ppermute | solution.py:282
  169.4 5.5 %collective-permute-start.34 = (bf16[112,768]{1,0:T(8,128)(2,1)S(1)}, bf16[112,768]{1,0:T(8,128)(2,1)S(1)}, u32[]{:S(2)}, u32[]{:S(2)}) collective-permute-start(bf16[112,768]{1,0:T(8,128)(2,1)S(1)} %fusion.31), channel_id=1, source_target_pairs={{0,8},{4,12},{8,0},{12,4},{16,24},{20,28},{24,16},{28,20},{1,9},{5... | collective-permute-start | bytes 516104 | tf_op jit(solution)/shard_map/ppermute | solution.py:186
  174.9 6.1 %collective-permute-start.35 = (bf16[112,768]{1,0:T(8,128)(2,1)S(1)}, bf16[112,768]{1,0:T(8,128)(2,1)S(1)}, u32[]{:S(2)}, u32[]{:S(2)}) collective-permute-start(bf16[112,768]{1,0:T(8,128)(2,1)S(1)} %collective-permute-done.34), channel_id=1, source_target_pairs={{0,1},{1,0},{2,3},{3,2},{4,5},{5,4},{6,7},{7,6},{8,9},{9,8},{10,11... | collective-permute-start | bytes 516104 | tf_op jit(solution)/shard_map/ppermute | solution.py:309
  177.9 5.4 %collective-permute-start.31 = (bf16[112,768]{1,0:T(8,128)(2,1)S(1)}, bf16[112,768]{1,0:T(8,128)(2,1)S(1)}, u32[]{:S(2)}, u32[]{:S(2)}) collective-permute-start(bf16[112,768]{1,0:T(8,128)(2,1)S(1)} %fusion.31), channel_id=1, source_target_pairs={{0,1},{1,0},{2,3},{3,2},{4,5},{5,4},{6,7},{7,6},{8,9},{9,8},{10,11... | collective-permute-start | bytes 516104 | tf_op jit(solution)/shard_map/ppermute | solution.py:308
  182.1 6.1 %copy-start.9 = (bf16[512,112]{1,0:T(8,128)(2,1)S(1)}, bf16[512,112]{1,0:T(8,128)(2,1)}, u32[]{:S(2)}) copy-start(bf16[512,112]{1,0:T(8,128)(2,1)} %copy-done.8) | copy-start | bytes 344068
  182.1 6.1 %collective-permute-start.36 = (bf16[112,1024]{1,0:T(8,128)(2,1)S(1)}, bf16[112,1024]{1,0:T(8,128)(2,1)S(1)}, u32[]{:S(2)}, u32[]{:S(2)}) collective-permute-start(bf16[112,1024]{1,0:T(8,128)(2,1)S(1)} %fusion.3), channel_id=1, source_target_pairs={{0,8},{4,12},{8,0},{12,4},{16,24},{20,28},{24,16},{28,20},{1,9},{5... | collective-permute-start | bytes 688136 | tf_op jit(solution)/shard_map/ppermute | solution.py:186
  183.3 8.0 %copy-start.1 = (bf16[512,2048]{1,0:T(8,128)(2,1)S(1)}, bf16[512,2048]{1,0:T(8,128)(2,1)}, u32[]{:S(2)}) copy-start(bf16[512,2048]{1,0:T(8,128)(2,1)} %param.17) | copy-start | bytes 6291460
  (13 other events, 41.0 us)
where the time goes:
time: 192 us; the launch traced here: 191 us
  waiting for transfers between devices  95.4 us (50%)
  starting transfers between devices  36.3 us (19%)
  Pallas kernels  27.4 us (14%)
  other arithmetic  15.7 us (8%)
  local copies, waits for them, and re-layouts  9.3 us (5%)
  matrix products  5.86 us (3%)
    ppermute x22, waiting for transfers between devices, swap(): return lax.ppermute(block, 'fsdp', pairs)  72.2 us
    ppermute x9, waiting for transfers between devices, fold(): return keep + lax.ppermute(step(give.astype(BF16)), axis, pairs).astype(F32)  19.4 us
    pallas_call x8, Pallas kernels, token_product(): pl.pallas_call(product_kernel, out_shape=jax.ShapeDtypeStruct((2 * rows,...  17.8 us
    ppermute x22, starting transfers between devices, swap(): return lax.ppermute(block, 'fsdp', pairs)  17.4 us
    ppermute x9, starting transfers between devices, fold(): return keep + lax.ppermute(step(give.astype(BF16)), axis, pairs).astype(F32)  8.67 us
    pallas_call x3, Pallas kernels, take_columns(): pl.pallas_call(functools.partial(take_kernel, rows, order), out_shape=(ha...  6.53 us
    ppermute x1, starting transfers between devices, on_line(): other = lax.ppermute(both, ('grp', 'tp'), ROUND)  4.43 us
    broadcast_in_dim x2, other arithmetic, on_line(): jnp.stack([g_all[i], up_all[i], d_all[i]], axis=1)[None]  4.13 us
  transfers between devices with their start and end apart: 37, of which 21 were waited for; matrix products, arithmetic and copies ran while one was open for 15% of the time, Pallas kernels for 9%

commit v1 on v0

v1 whole, which is shorter than its diff:
```python
import functools

import jax
import jax.numpy as jnp
from jax import lax
from jax.experimental import pallas as pl
from jax.experimental.pallas import tpu as pltpu
from jax.sharding import PartitionSpec as P

CAP = 112

first_decay = 0.9
second_decay = 0.95
first_fix = 1.0 - 0.9**10
second_fix = 1.0 - 0.95**10
learn_rate = 0.002
weight_decay = 0.1
epsilon = 1e-08

F32 = jnp.float32
BF16 = jnp.bfloat16
SMALL = pl.CostEstimate(flops=0, bytes_accessed=0, transcendentals=0)
BY_TOKENS = (((0,), (0,)), ((), ()))
BY_LAST = (((1,), (1,)), ((), ()))

CORES = [(i, i ^ 1) for i in range(8)]
NEAR = [(i, i ^ 2) for i in range(8)]
FAR = [(i, i ^ 4) for i in range(8)]
SWAP = [(0, 1), (1, 0)]
NEAR_TURNED = [(i, i ^ 5) for i in range(16)]
TURN = [(0, 0), (1, 2), (2, 1), (3, 3)]
ROUND = [(0, 1), (1, 3), (3, 2), (2, 0)]


def activations(preact, hidden_cot):
    gate_pre = preact[:, 0, :].astype(F32)
    up_pre = preact[:, 1, :].astype(F32)
    logistic = jax.nn.sigmoid(gate_pre)
    activated = gate_pre * logistic
    hidden_act = (activated * up_pre).astype(BF16)
    cotangent = hidden_cot.astype(F32)
    grad_gate = (cotangent * up_pre * logistic * (1.0 + gate_pre * (1.0 - logistic))).astype(BF16)
    grad_up = (cotangent * activated).astype(BF16)
    return hidden_act, grad_gate, grad_up


def adam(master, moment, second, grad):
    moment_new = first_decay * moment + (1.0 - first_decay) * grad
    second_new = second_decay * second + (1.0 - second_decay) * grad * grad
    step_size = moment_new / first_fix / (jnp.sqrt(second_new / second_fix) + epsilon)
    master_new = master - learn_rate * (step_size + weight_decay * master)
    return master_new, moment_new, second_new


def slots(routes, route_weight):
    named = routes == 0
    chosen_row = jnp.any(named, axis=1)
    slot_of_row = jnp.cumsum(chosen_row.astype(jnp.int32)) - 1
    place = slot_of_row[:, None] == jnp.arange(CAP, dtype=jnp.int32)[None, :]
    place = (place & chosen_row[:, None]).astype(BF16)
    return place, jnp.sum(jnp.where(named, route_weight, 0.0), axis=1, keepdims=True)


def pick(place, rollout_in):
    return lax.dot_general(place, rollout_in, BY_TOKENS, preferred_element_type=F32).astype(BF16)


def near_first(i):
    return i


def far_first(i):
    return ((i & 1) << 1) | (i >> 1)


def take_kernel(rows, order, place_ref, source, *targets):
    for t, target in enumerate(targets):
        core = place_ref[1] if t else 1 - place_ref[1]
        for i in range(4):
            block = 2 * (place_ref[0] ^ order(i)) + core
            start = pl.multiple_of(block * rows, rows)
            target[:, i * rows : (i + 1) * rows] = source[:, pl.ds(start, rows)]


def take_columns(array, rows, order, count, place):
    half = jax.ShapeDtypeStruct((array.shape[0], 4 * rows), array.dtype)
    return pl.pallas_call(
        functools.partial(take_kernel, rows, order),
        out_shape=(half,) * count,
        in_specs=[
            pl.BlockSpec(memory_space=pltpu.SMEM),
            pl.BlockSpec(memory_space=pltpu.VMEM),
        ],
        out_specs=(pl.BlockSpec(memory_space=pltpu.VMEM),) * count,
        cost_estimate=SMALL,
    )(place, array)


def product_kernel(place_ref, *refs):
    own_pre, got_pre, *refs = refs
    count = len(refs) // 3
    for own, got, out in zip(refs[:count], refs[count : 2 * count], refs[2 * count :]):
        total = lax.dot_general(own[...], own_pre[...], BY_TOKENS, preferred_element_type=F32)
        total += lax.dot_general(got[...], got_pre[...], BY_TOKENS, preferred_element_type=F32)
        out[...] = total.astype(out.dtype)


def token_products(own, got, own_pre, got_pre, place, firsts, span, dtypes):
    tokens = own_pre.shape[0]
    rows = got.shape[1] // 4
    width = span.stop - span.start
    pre = pl.BlockSpec((tokens, width), lambda i, p: (0, span.start // width))

    def own_block(first):
        return lambda i, p: (0, 2 * (p[0] ^ far_first(first)) + p[1])

    def got_block(first):
        return lambda i, p: (0, first)

    blocks = [pl.BlockSpec((tokens, rows), own_block(first)) for first in firsts]
    blocks += [pl.BlockSpec((tokens, rows), got_block(first)) for first in firsts]
    outs = tuple(jax.ShapeDtypeStruct((rows, width), dtype) for dtype in dtypes)
    return pl.pallas_call(
        product_kernel,
        out_shape=outs,
        grid_spec=pltpu.PrefetchScalarGridSpec(
            num_scalar_prefetch=1,
            grid=(1,),
            in_specs=[pre, pre] + blocks,
            out_specs=tuple(pl.BlockSpec((rows, width), lambda i, p: (0, 0)) for _ in outs),
        ),
        compiler_params=pltpu.CompilerParams(vmem_limit_bytes=32 << 20),
        cost_estimate=SMALL,
    )(place, own_pre, got_pre, *[own] * len(firsts), *[got] * len(firsts))


def spread_kernel(place_ref, slots, weight, values, out):
    rows = out.shape[1] // 8
    for i in range(8):
        unit = place_ref[0] ^ ((i >> 2) | ((i & 1) << 1))
        block = 2 * unit + (place_ref[1] ^ ((i >> 1) & 1))
        placed = jnp.dot(
            slots[...], values[:, i * rows : (i + 1) * rows], preferred_element_type=F32
        )
        start = pl.multiple_of(block * rows, rows)
        out[:, pl.ds(start, rows)] = (weight[...] * placed).astype(out.dtype)


def spread(values, slots, weight, place):
    count, width = slots.shape[0], values.shape[1]
    step = count // 4
    return pl.pallas_call(
        spread_kernel,
        out_shape=jax.ShapeDtypeStruct((count, width), BF16),
        grid_spec=pltpu.PrefetchScalarGridSpec(
            num_scalar_prefetch=1,
            grid=(4,),
            in_specs=[
                pl.BlockSpec((step, CAP), lambda i, p: (i, 0)),
                pl.BlockSpec((step, 1), lambda i, p: (i, 0)),
                pl.BlockSpec((CAP, width), lambda i, p: (0, 0)),
            ],
            out_specs=pl.BlockSpec((step, width), lambda i, p: (i, 0)),
        ),
        compiler_params=pltpu.CompilerParams(vmem_limit_bytes=32 << 20),
        cost_estimate=SMALL,
    )(place, slots, weight, values)


def row_kernel(place_ref, picked, there, *targets):
    rows = picked.shape[1] // 8
    chip, core = place_ref[0], place_ref[1]
    for target, parity in zip(targets, (1 - core, core)):
        for i in range(2):
            unit = chip ^ i
            start = pl.multiple_of((2 * unit + parity) * rows, rows)
            target[0, :, i * rows : (i + 1) * rows] = picked[:, pl.ds(start, rows)]
            start = pl.multiple_of((2 * (unit & 1) + parity) * rows, rows)
            target[1, :, i * rows : (i + 1) * rows] = there[:, pl.ds(start, rows)]


def split_rows(picked, there, rows, place):
    shape = jax.ShapeDtypeStruct((2, CAP, 2 * rows), BF16)
    return pl.pallas_call(
        row_kernel,
        out_shape=(shape, shape),
        in_specs=[
            pl.BlockSpec(memory_space=pltpu.SMEM),
            pl.BlockSpec(memory_space=pltpu.VMEM),
            pl.BlockSpec(memory_space=pltpu.VMEM),
        ],
        out_specs=(pl.BlockSpec(memory_space=pltpu.VMEM),) * 2,
        cost_estimate=SMALL,
    )(place, picked, there)


def on_line(
    learn_in,
    learn_cot,
    preact,
    hidden_cot,
    master,
    moment,
    second,
    rollout_in,
    routes,
    route_weight,
):
    index = lax.axis_index("fsdp")
    grp = lax.axis_index("grp")
    tp = lax.axis_index("tp")
    line = jnp.stack([index // 2, index % 2])
    rows = master.shape[1]
    width = preact.shape[2]
    last = None

    def send(name, block, axis, pairs):
        with jax.named_scope(name):
            return lax.ppermute(block, axis, pairs)

    def step(work, *operands):
        nonlocal last
        if last is not None:
            operands = lax.optimization_barrier((*operands, last))[:-1]
        done = work(*operands)
        last = done[0] if isinstance(done, tuple) else done
        return done

    def mark(done):
        nonlocal last
        several = isinstance(done, tuple)
        done = done if several else (done,)
        if last is not None:
            done = lax.optimization_barrier((*done, last))[:-1]
        last = done[0]
        return done if several else done[0]

    def hold(array):
        return lax.optimization_barrier((array, last))[0]

    def wait(array):
        nonlocal last
        array, last = lax.optimization_barrier((array, last))
        return array

    diagonal = grp == tp

    whole = slice(0, width)

    def give(order, count):
        return lambda array: take_columns(array, rows, order, count, line)

    def token_sums(first, span, dtype):
        return lambda *args: token_products(*args, line, first, span, dtype)

    def given_sum(own, other):
        return (own + other.astype(F32)).astype(BF16)

    def update(which, span):
        def work(own, near, across):
            total = own + near.astype(F32) + across.astype(F32)
            old = [array[0, :, which, span] for array in (master, moment, second)]
            new = adam(*old, total)
            return (new[0].astype(BF16), *new)

        return work

    def activated(preact, hidden_cot):
        return activations(preact, hidden_cot)[0]

    def pre_grads(preact, hidden_cot):
        return activations(preact, hidden_cot)[1:]

    def far_rows(picked):
        return lax.dynamic_slice_in_dim(picked, (1 - index // 4) * 4 * rows, 4 * rows, 1)

    def take_rows(picked, there):
        return split_rows(picked, there, rows, line)

    def both_cores(keep, got):
        return jnp.stack([keep, got])

    def plane_rows(turned, other):
        mine = jnp.where(diagonal, turned, other)
        theirs = jnp.where(diagonal, other, turned)
        by_grp, by_chip = jnp.stack([mine, theirs], axis=1), jnp.stack([mine, theirs], axis=2)
        return by_grp.reshape(-1, 2 * rows), by_chip.reshape(-1, 2 * rows)

    def joined(*blocks):
        return jnp.concatenate(blocks)

    def relayed(block, vertical):
        return jnp.where(diagonal, vertical, block)

    def plane_weights(*blocks):
        halves = [
            jnp.concatenate([jnp.where(diagonal, block, vertical), horizontal], axis=1)
            for block, vertical, horizontal in (blocks[:3], blocks[3:])
        ]
        return jnp.concatenate(halves)

    def stacked(*news):
        return tuple(jnp.stack(news[i::3], axis=1)[None] for i in range(3))

    def slot_product(slot_rows, left, right):
        total = jnp.dot(slot_rows[:, :rows], left, preferred_element_type=F32)
        total += jnp.dot(slot_rows[:, rows:], right, preferred_element_type=F32)
        keep, give = jnp.split(total, 2)
        return give.astype(BF16), keep

    def folded(kept, got):
        keep, give = jnp.split(kept + got.astype(F32), 2)
        return give.astype(BF16), keep

    def activate(*parts):
        sums = [kept + got.astype(F32) for kept, got in zip(parts[::2], parts[1::2])]
        up = jnp.concatenate(sums[1:], axis=1)
        return (jax.nn.silu(sums[0]) * up).astype(BF16)

    def down_product(left, right, near, far):
        slots = jnp.concatenate([left, right], axis=1)
        down = jnp.concatenate([near, far])
        return lax.dot_general(slots, down, BY_LAST, preferred_element_type=F32).astype(BF16)

    (cot_give,) = mark(give(far_first, 1)(learn_cot))
    cot_got = send("cot_got", cot_give, "fsdp", CORES)
    act = mark(activated(preact, hidden_cot))
    act_got = send("act_got", act, "fsdp", CORES)
    (d_gb,) = mark(token_sums((3,), whole, (BF16,))(learn_cot, cot_got, act, act_got))
    d_b = send("d_b", d_gb, "fsdp", NEAR)
    place, weight = mark(slots(routes, route_weight))
    picked = mark(pick(place, rollout_in))
    picked_far = mark(far_rows(picked))
    there = send("there", picked_far, "fsdp", FAR)
    (in_give,) = mark(give(far_first, 1)(learn_in))
    in_got = send("in_got", in_give, "fsdp", CORES)
    gate, up = mark(pre_grads(preact, hidden_cot))
    gate_got = send("gate_got", gate, "fsdp", CORES)
    up_got = send("up_got", up, "fsdp", CORES)
    g_gb, g_kb = mark(token_sums((3, 1), whole, (BF16, F32))(learn_in, in_got, gate, gate_got))
    d_ga, d_ka = mark(token_sums((2, 0), whole, (BF16, F32))(learn_cot, cot_got, act, act_got))
    d_a = send("d_a", d_ga, "fsdp", NEAR)
    g_b = send("g_b", g_gb, "fsdp", NEAR)
    (d_kb,) = mark(token_sums((1,), whole, (F32,))(learn_cot, cot_got, act, act_got))
    g_ga, g_ka = mark(token_sums((2, 0), whole, (BF16, F32))(learn_in, in_got, gate, gate_got))
    g_a = send("g_a", g_ga, "fsdp", NEAR)
    d_x = mark(given_sum(d_kb, d_b))
    d_across = send("d_across", d_x, "fsdp", FAR)
    g_x = mark(given_sum(g_kb, g_b))
    g_across = send("g_across", g_x, "fsdp", FAR)
    row_give, row_keep = mark(take_rows(picked, there))
    row_got = send("row_got", row_give, "fsdp", CORES)
    u_gb, u_kb = mark(token_sums((3, 1), whole, (BF16, F32))(learn_in, in_got, up, up_got))
    u_b = send("u_b", u_gb, "fsdp", NEAR)
    both = mark(both_cores(row_keep, row_got))
    turned = send("turned", both, ("grp", "tp"), TURN)
    rotated = send("rotated", both, ("grp", "tp"), ROUND)
    d_shard, *d_all = mark(update(2, whole)(d_ka, d_a, d_across))
    d_other = send("d_other", d_shard, "fsdp", FAR)
    vert_z = send("vert_z", d_shard, "grp", SWAP)
    g_shard, *g_all = mark(update(0, whole)(g_ka, g_a, g_across))
    g_near = send("g_near", g_shard, "fsdp", NEAR)
    u_x = mark(given_sum(u_kb, u_b))
    u_across = send("u_across", u_x, "fsdp", FAR)
    u_ga, u_ka = mark(token_sums((2, 0), whole, (BF16, F32))(learn_in, in_got, up, up_got))
    u_a = send("u_a", u_ga, "fsdp", NEAR)
    relay_z = mark(relayed(d_shard, vert_z))
    hori_z = send("hori_z", relay_z, "tp", SWAP)
    slot_rows, slot_rows_g = mark(plane_rows(turned, rotated))
    g_core, g_half = mark(slot_product(slot_rows_g, g_shard, g_near))
    g_core_got = send("g_core_got", g_core, "fsdp", CORES)
    g_far, g_quarter = mark(folded(g_half, g_core_got))
    g_far_got = send("g_far_got", g_far, "fsdp", FAR)
    u_shard, *u_all = mark(update(1, whole)(u_ka, u_a, u_across))
    u_near = send("u_near", u_shard, "fsdp", NEAR)
    d_other = wait(d_other)
    vert_f = send("vert_f", hold(d_other), "grp", SWAP)
    master_new, moment_new, second_new = mark(stacked(*g_all, *u_all, *d_all))
    hori_z = wait(hori_z)
    u_core, u_half = step(slot_product, slot_rows, u_shard, u_near)
    u_core_got = send("u_core_got", u_core, "fsdp", CORES)
    u_grp, u_quarter = step(folded, u_half, u_core_got)
    u_grp_got = send("u_grp_got", u_grp, "grp", SWAP)
    relay_f = step(relayed, d_other, vert_f)
    hori_f = send("hori_f", relay_f, "tp", SWAP)
    u_far, u_sum = step(folded, u_quarter, u_grp_got)
    u_far_got = send("u_far_got", u_far, "fsdp", FAR)
    g_grp, g_sum = step(folded, g_quarter, g_far_got)
    g_grp_got = send("g_grp_got", g_grp, "grp", SWAP)
    down = step(plane_weights, d_shard, vert_z, hori_z, d_other, vert_f, hori_f)
    down_got = send("down_got", down, "fsdp", CORES)
    hidden = mark(activate(g_sum, g_grp_got, u_sum, u_far_got))
    near_hidden = send("near_hidden", hidden, "fsdp", NEAR)
    near_turned = send("near_turned", hidden, ("fsdp", "tp"), NEAR_TURNED)
    beside = send("beside", hidden, "tp", SWAP)
    near_out = mark(down_product(near_hidden, near_turned, down, down_got))
    near_out_got = send("near_out_got", near_out, "fsdp", NEAR)
    out = mark(down_product(hidden, beside, down, down_got))

    slot_out = jnp.concatenate([out, near_out_got], axis=1)
    expert_out = spread(slot_out, place, weight, line)
    return (master_new, moment_new, second_new, expert_out)


def on_device(
    learn_in,
    learn_cot,
    preact,
    hidden_cot,
    master,
    moment,
    second,
    rollout_in,
    routes,
    route_weight,
):
    hidden_width = preact.shape[2]
    hidden_act, grad_gate, grad_up = activations(preact, hidden_cot)
    pre_grads = jnp.concatenate([grad_gate, grad_up], axis=1)
    front = lax.dot_general(
        learn_in, pre_grads, BY_TOKENS, preferred_element_type=F32
    ).reshape(master.shape[1] * lax.axis_size("fsdp"), 2, hidden_width)
    back = lax.dot_general(learn_cot, hidden_act, BY_TOKENS, preferred_element_type=F32)[:, None, :]
    grad = lax.psum_scatter(
        jnp.concatenate([front, back], axis=1).astype(BF16),
        "fsdp",
        scatter_dimension=0,
        tiled=True,
    ).astype(F32)[None]
    master_new, moment_new, second_new = adam(master, moment, second, grad)
    half_rows = lax.all_gather(master_new.astype(BF16), "fsdp", axis=1, tiled=True)
    passed = lax.all_gather(half_rows, "grp", axis=0, tiled=True).reshape(-1, 3, hidden_width)
    weight_in = passed[:, :2, :].reshape(-1, 2 * hidden_width)
    place, weight = slots(routes, route_weight)
    slot_rows = lax.all_gather(pick(place, rollout_in), "tp", axis=1, tiled=True)
    slot_pre = jnp.dot(slot_rows, weight_in, preferred_element_type=F32)
    slot_hidden = jax.nn.silu(slot_pre[:, :hidden_width]) * slot_pre[:, hidden_width:]
    partial_out = lax.dot_general(
        slot_hidden.astype(BF16), passed[:, 2, :], BY_LAST, preferred_element_type=F32
    )
    slot_out = lax.psum_scatter(
        partial_out.astype(BF16), "tp", scatter_dimension=1, tiled=True
    )
    placed = jnp.dot(place, slot_out, preferred_element_type=F32)
    expert_out = (weight * placed).astype(BF16)
    return (master_new, moment_new, second_new, expert_out)


def solution(mesh):
    in_specs = (
        P("fsdp", "grp"),
        P("fsdp", "grp"),
        P("fsdp", None, "tp"),
        P("fsdp", "tp"),
        P("grp", "fsdp", None, "tp"),
        P("grp", "fsdp", None, "tp"),
        P("grp", "fsdp", None, "tp"),
        P(("fsdp", "grp"), "tp"),
        P(("fsdp", "grp"), None),
        P(("fsdp", "grp"), None),
    )
    out_specs = (
        P("grp", "fsdp", None, "tp"),
        P("grp", "fsdp", None, "tp"),
        P("grp", "fsdp", None, "tp"),
        P(("fsdp", "grp"), "tp"),
    )
    small = (mesh.shape["fsdp"], mesh.shape["grp"], mesh.shape["tp"]) == (8, 2, 2)
    return jax.shard_map(
        on_line if small else on_device,
        mesh=mesh,
        in_specs=in_specs,
        out_specs=out_specs,
        check_vma=False,
    )
```

time: 192 us -> 186 us (0.969)
  waiting for transfers between devices: 95.4 us -> 83.9 us
  starting transfers between devices: 36.3 us -> 45.1 us
  local copies, waits for them, and re-layouts: 9.3 us -> 5.26 us
  matrix products: 5.86 us -> 8.01 us
    ppermute x37 -> x36, waiting for transfers between devices: 95.4 us -> 83.9 us  [send(): return lax.ppermute(block, axis, pairs)]
    ppermute x37 -> x36, starting transfers between devices: 36.3 us -> 45.1 us  [send(): return lax.ppermute(block, axis, pairs)]
    slice x9 -> x1, local copies, waits for them, and re-layouts: 4.91 us -> 0.07 us  [the longest x2 2.01 us: on_line(): u_args = (learn_in, in_got, grad_up[:, :cut], got_up[:, :cut])]
    add x12 -> x4, other arithmetic: 3.29 us -> 0.46 us  [folded(): keep, give = jnp.split(kept + got.astype(F32), 2)]
    dot_general x9 -> x7, matrix products: 5.86 us -> 8.01 us  [the longest x2 5.44 us: down_product(): lax.dot_general(slots, down, BY_LAST, preferred_element_type=F32)]
    pallas_call x3 -> x2, Pallas kernels: 6.53 us -> 4.65 us  [take_columns(): pl.pallas_call(functools.partial(take_kernel, rows, order), out_shape=(ha...]
    convert_element_type x5 -> x6, other arithmetic: 3.64 us -> 5.42 us  [the longest x2 3.54 us: work(): return (new[0].astype(BF16), *new)]
    broadcast_in_dim x2 -> x3, other arithmetic: 4.13 us -> 4.67 us  [stacked(): return tuple((jnp.stack(news[i::3], axis=1)[None] for i in range(3)))]
  transfers between devices with their start and end apart: 37 -> 36, of which waited for: 21 -> 15; matrix products, arithmetic and copies ran while one was open for 15% -> 13% of each run, Pallas kernels for 9% -> 10%
where the time goes in v1:
time: 186 us
  waiting for transfers between devices  83.9 us (45%)
  starting transfers between devices  45.1 us (24%)
  Pallas kernels  27.2 us (15%)
  other arithmetic  15.2 us (8%)
  matrix products  8.01 us (4%)
  local copies, waits for them, and re-layouts  5.26 us (3%)
    ppermute x36, waiting for transfers between devices, send(): return lax.ppermute(block, axis, pairs)  83.9 us
    ppermute x36, starting transfers between devices, send(): return lax.ppermute(block, axis, pairs)  45.1 us
    pallas_call x7, Pallas kernels, token_products(): pl.pallas_call(product_kernel, out_shape=outs, grid_spec=pltpu.PrefetchSc...  17.5 us
    dot_general x2, matrix products, down_product(): lax.dot_general(slots, down, BY_LAST, preferred_element_type=F32)  5.44 us
    broadcast_in_dim x3, other arithmetic, stacked(): return tuple((jnp.stack(news[i::3], axis=1)[None] for i in range(3)))  4.67 us
    pallas_call x2, Pallas kernels, take_columns(): pl.pallas_call(functools.partial(take_kernel, rows, order), out_shape=(ha...  4.65 us
  transfers between devices with their start and end apart: 36, of which 15 were waited for; matrix products, arithmetic and copies ran while one was open for 13% of the time, Pallas kernels for 10%

profile of v1, /device:TPU:0, one launch (start us, length us, event | category | flops | bytes accessed | tf_op | source)
XLA Modules:
  0.0 186.0 jit_solution(13455271985211606386)
XLA Ops:
  1.3 2.3 %shard_map.130 = bf16[344,1024]{1,0:T(8,128)(2,1)} custom-call(s32[2]{0:T(128)} %pad_add_fusion.place_ref, bf16[344,2048]{1,0:T(8,128)(2,1)} %refs_3_.6), custom_call_target="tpu_custom_call" | custom-call | tf_op jit(solution)/shard_map/pallas_call | solution.py:87
  4.0 1.5 fusion.46
  5.6 1.8 fusion.3
  7.5 2.3 %shard_map.129 = bf16[344,1024]{1,0:T(8,128)(2,1)} custom-call(s32[2]{0:T(128)} %pad_add_fusion.place_ref, bf16[344,2048]{1,0:T(8,128)(2,1)} %refs_3_.9), custom_call_target="tpu_custom_call" | custom-call | tf_op jit(solution)/shard_map/pallas_call | solution.py:87
  10.7 2.4 %shard_map.131 = bf16[256,768]{1,0:T(8,128)(2,1)S(1)} custom-call(s32[2]{0:T(128)S(1)} %copy-done.13, bf16[344,768]{1,0:T(8,128)(2,1)} %get-tuple-element.87.refs_0_, bf16[344,768]{1,0:T(8,128)(2,1)} %collective-permute-done.refs_1_, bf16[344,2048]{1,0:T(8,128)(2,1)S(1)} %copy-done.3, bf16[344,1024]{1,0:T(8,128)(2,1)} %collective-permute-done.1.refs_3_.refs_4_.refs_5_), custom_call_target="tpu_custom_call" | custom-call | tf_op jit(solution)/shard_map/pallas_call | solution.py:123
  14.9 2.9 %collective-permute-start.6 = (bf16[256,768]{1,0:T(8,128)(2,1)S(1)}, bf16[256,768]{1,0:T(8,128)(2,1)S(1)}, u32[]{:S(2)}, u32[]{:S(2)}) collective-permute-start(bf16[256,768]{1,0:T(8,128)(2,1)S(1)} %shard_map.131), channel_id=1, source_target_pairs={{0,8},{4,12},{8,0},{12,4},{16,24},{20,28},{24,16},{28,20},{1,9},{5... | collective-permute-start | bytes 1179656 | tf_op jit(solution)/shard_map/d_b/ppermute | solution.py:219
  17.8 1.6 shard_map.135
  19.4 2.4 %collective-permute-start.5 = (bf16[256,768]{1,0:T(8,128)(2,1)S(1)}, bf16[256,768]{1,0:T(8,128)(2,1)S(1)}, u32[]{:S(2)}, u32[]{:S(2)}) collective-permute-start(bf16[256,768]{1,0:T(8,128)(2,1)S(1)} %get-tuple-element.100), channel_id=1, source_target_pairs={{0,8},{4,12},{8,0},{12,4},{16,24},{20,28},{24,16},{28,20},{1,9},{5... | collective-permute-start | bytes 1179656 | tf_op jit(solution)/shard_map/g_b/ppermute | solution.py:219
  21.8 2.6 %collective-permute-start.10 = (bf16[112,1024]{1,0:T(8,128)(2,1)S(1)}, bf16[112,1024]{1,0:T(8,128)(2,1)S(1)}, u32[]{:S(2)}, u32[]{:S(2)}) collective-permute-start(bf16[112,1024]{1,0:T(8,128)(2,1)S(1)} %constant_dynamic-slice_fusion), channel_id=1, source_target_pairs={{0,16},{4,20},{8,24},{12,28},{16,0},{20,4},{24,8},{28,12},{1,17},{... | collective-permute-start | bytes 688136 | tf_op jit(solution)/shard_map/there/ppermute | solution.py:219
  24.4 2.4 %shard_map.133 = f32[256,768]{1,0:T(8,128)S(1)} custom-call(s32[2]{0:T(128)S(1)} %copy-done.13, bf16[344,768]{1,0:T(8,128)(2,1)} %get-tuple-element.87.refs_0_, bf16[344,768]{1,0:T(8,128)(2,1)} %collective-permute-done.refs_1_, bf16[344,2048]{1,0:T(8,128)(2,1)S(1)} %copy-done.4, bf16[344,1024]{1,0:T(8,128)(2,1)} %collective-permute-done.1.refs_3_.refs_4_.refs_5_), custom_call_target="tpu_custom_call" | custom-call | tf_op jit(solution)/shard_map/pallas_call | solution.py:123
  26.8 3.3 %shard_map.134 = (bf16[256,768]{1,0:T(8,128)(2,1)}, f32[256,768]{1,0:T(8,128)S(1)}) custom-call(s32[2]{0:T(128)S(1)} %copy-done.13, bf16[344,768]{1,0:T(8,128)(2,1)} %get-tuple-element.87.refs_0_, bf16[344,768]{1,0:T(8,128)(2,1)} %collective-permute-done.refs_1_, bf16[344,2048]{1,0:T(8,128)(2,1)S(1)} %copy-done.4, bf16[344,2048]{1,0:T(8,128)(2,1)S(1)} %copy-done.4, ...), custom_call_target="tpu_custom_call" | custom-call | tf_op jit(solution)/shard_map/pallas_call | solution.py:123
  31.5 2.0 %shard_map.132 = (bf16[256,768]{1,0:T(8,128)(2,1)}, f32[256,768]{1,0:T(8,128)S(1)}) custom-call(s32[2]{0:T(128)S(1)} %copy-done.13, bf16[344,768]{1,0:T(8,128)(2,1)S(1)} %copy-done.6, bf16[344,768]{1,0:T(8,128)(2,1)S(1)} %collective-permute-done.2.refs_1_, bf16[344,2048]{1,0:T(8,128)(2,1)S(1)} %copy-done.2, bf16[344,2048]{1,0:T(8,128)(2,1)S(1)} %copy-done.2, ...), custom_call_target="tpu_custom_call" | custom-call | tf_op jit(solution)/shard_map/pallas_call | solution.py:123
  33.6 1.5 collective-permute-start.4
  35.9 5.1 %collective-permute-done.5 = bf16[256,768]{1,0:T(8,128)(2,1)S(1)} collective-permute-done((bf16[256,768]{1,0:T(8,128)(2,1)S(1)}, bf16[256,768]{1,0:T(8,128)(2,1)S(1)}, u32[]{:S(2)}, u32[]{:S(2)}) %collective-permute-start.5) | collective-permute-done | bytes 393248 | tf_op jit(solution)/shard_map/g_b/ppermute | solution.py:219
  41.1 2.2 %collective-permute-start.9 = (bf16[256,768]{1,0:T(8,128)(2,1)}, bf16[256,768]{1,0:T(8,128)(2,1)}, u32[]{:S(2)}, u32[]{:S(2)}) collective-permute-start(bf16[256,768]{1,0:T(8,128)(2,1)} %add_convert_fusion.1), channel_id=1, source_target_pairs={{0,16},{4,20},{8,24},{12,28},{16,0},{20,4},{24,8},{28,12},{1,17},{... | collective-permute-start | bytes 1179656 | tf_op jit(solution)/shard_map/d_across/ppermute | solution.py:219
  45.5 1.9 %shard_map.136 = (bf16[2,112,512]{2,1,0:T(8,128)(2,1)}, bf16[2,112,512]{2,1,0:T(8,128)(2,1)}) custom-call(s32[2]{0:T(128)} %pad_add_fusion.place_ref, bf16[112,2048]{1,0:T(8,128)(2,1)} %copy-done.17, bf16[112,1024]{1,0:T(8,128)(2,1)} %copy-done.27), custom_call_target="tpu_custom_call" | custom-call | tf_op jit(solution)/shard_map/pallas_call | solution.py:184
  47.5 2.9 %shard_map.137 = (bf16[256,768]{1,0:T(8,128)(2,1)S(1)}, f32[256,768]{1,0:T(8,128)S(1)}) custom-call(s32[2]{0:T(128)S(1)} %copy-done.14, bf16[344,768]{1,0:T(8,128)(2,1)S(1)} %copy-done.5, bf16[344,768]{1,0:T(8,128)(2,1)} %collective-permute-done.12.refs_1_, bf16[344,2048]{1,0:T(8,128)(2,1)S(1)} %copy-done.2, bf16[344,2048]{1,0:T(8,128)(2,1)S(1)} %copy-done.2, ...), custom_call_target="tpu_custom_call" | custom-call | tf_op jit(solution)/shard_map/pallas_call | solution.py:123
  50.4 3.0 %shard_map.138 = (bf16[256,768]{1,0:T(8,128)(2,1)S(1)}, f32[256,768]{1,0:T(8,128)S(1)}) custom-call(s32[2]{0:T(128)S(1)} %copy-done.14, bf16[344,768]{1,0:T(8,128)(2,1)S(1)} %copy-done.5, bf16[344,768]{1,0:T(8,128)(2,1)} %collective-permute-done.12.refs_1_, bf16[344,2048]{1,0:T(8,128)(2,1)S(1)} %copy-done.2, bf16[344,2048]{1,0:T(8,128)(2,1)S(1)} %copy-done.2, ...), custom_call_target="tpu_custom_call" | custom-call | tf_op jit(solution)/shard_map/pallas_call | solution.py:123
  53.4 1.8 collective-permute-start.13
  56.2 17.6 %collective-permute-done.4 = bf16[256,768]{1,0:T(8,128)(2,1)} collective-permute-done((bf16[256,768]{1,0:T(8,128)(2,1)}, bf16[256,768]{1,0:T(8,128)(2,1)}, u32[]{:S(2)}, u32[]{:S(2)}) %collective-permute-start.4) | collective-permute-done | bytes 393248 | tf_op jit(solution)/shard_map/g_a/ppermute | solution.py:219
  74.5 5.1 %collective-permute-start.17 = (bf16[2,2,112,512]{3,2,1,0:T(8,128)(2,1)S(1)}, bf16[2,2,112,512]{3,2,1,0:T(8,128)(2,1)S(1)}, u32[]{:S(2)}, u32[]{:S(2)}) collective-permute-start(bf16[2,2,112,512]{3,2,1,0:T(8,128)(2,1)S(1)} %pad_maximum_fusion.3), channel_id=1, source_target_pairs={{0,1},{1,3},{3,2},{2,0},{4,5},{5,7},{7,6},{6,4},{8,9},{9,11},{11,1... | collective-permute-start | bytes 1376264 | tf_op jit(solution)/shard_map/rotated/ppermute | solution.py:219
  79.6 2.8 %fusion.42 = (bf16[256,768]{1,0:T(8,128)(2,1)S(1)}, f32[256,768]{1,0:T(8,128)S(1)}, f32[256,768]{1,0:T(8,128)S(1)}, f32[256,768]{1,0:T(8,128)S(1)}, bf16[256,768...) fusion(f32[1,256,3,768]{3,1,2,0:T(8,128)S(1)} %copy-done.18, ...), kind=kLoop, calls=%fused_computation.107 | loop fusion | flops 7864320 | bytes 13369344 | tf_op jit(solution)/shard_map/convert_element_type | solution.py:264
  83.0 3.5 %collective-permute-start.15 = (bf16[256,768]{1,0:T(8,128)(2,1)S(1)}, bf16[256,768]{1,0:T(8,128)(2,1)S(1)}, u32[]{:S(2)}, u32[]{:S(2)}) collective-permute-start(bf16[256,768]{1,0:T(8,128)(2,1)S(1)} %add_convert_fusion), channel_id=1, source_target_pairs={{0,16},{4,20},{8,24},{12,28},{16,0},{20,4},{24,8},{28,12},{1,17},{... | collective-permute-start | bytes 1179656 | tf_op jit(solution)/shard_map/u_across/ppermute | solution.py:219
  86.5 1.5 collective-permute-start.14
  88.0 3.0 %collective-permute-done.17 = bf16[2,2,112,512]{3,2,1,0:T(8,128)(2,1)S(1)} collective-permute-done((bf16[2,2,112,512]{3,2,1,0:T(8,128)(2,1)S(1)}, bf16[2,2,112,512]{3,2,1,0:T(8,128)(2,1)S(1)}, u32[]{:S(2)}, u32[]{:S(2)}) %collective-permute-start.17) | collective-permute-done | bytes 458784 | tf_op jit(solution)/shard_map/rotated/ppermute | solution.py:219
  91.5 5.4 %collective-permute-done.18 = bf16[256,768]{1,0:T(8,128)(2,1)S(1)} collective-permute-done((bf16[256,768]{1,0:T(8,128)(2,1)S(1)}, bf16[256,768]{1,0:T(8,128)(2,1)S(1)}, u32[]{:S(2)}, u32[]{:S(2)}) %collective-permute-start.18) | collective-permute-done | bytes 393248 | tf_op jit(solution)/shard_map/vert_z/ppermute | solution.py:219
  97.5 5.5 %collective-permute-done.19 = bf16[256,768]{1,0:T(8,128)(2,1)S(1)} collective-permute-done((bf16[256,768]{1,0:T(8,128)(2,1)S(1)}, bf16[256,768]{1,0:T(8,128)(2,1)S(1)}, u32[]{:S(2)}, u32[]{:S(2)}) %collective-permute-start.19) | collective-permute-done | bytes 393248 | tf_op jit(solution)/shard_map/g_near/ppermute | solution.py:219
  103.8 4.6 %collective-permute-done.14 = bf16[256,768]{1,0:T(8,128)(2,1)S(1)} collective-permute-done((bf16[256,768]{1,0:T(8,128)(2,1)S(1)}, bf16[256,768]{1,0:T(8,128)(2,1)S(1)}, u32[]{:S(2)}, u32[]{:S(2)}) %collective-permute-start.14) | collective-permute-done | bytes 393248 | tf_op jit(solution)/shard_map/u_a/ppermute | solution.py:219
  110.9 2.5 %collective-permute-start.25 = (bf16[256,768]{1,0:T(8,128)(2,1)S(1)}, bf16[256,768]{1,0:T(8,128)(2,1)S(1)}, u32[]{:S(2)}, u32[]{:S(2)}) collective-permute-start(bf16[256,768]{1,0:T(8,128)(2,1)S(1)} %get-tuple-element.160), channel_id=1, source_target_pairs={{0,16},{4,20},{8,24},{12,28},{16,0},{20,4},{24,8},{28,12},{1,17},{... | collective-permute-start | bytes 1179656 | tf_op jit(solution)/shard_map/d_other/ppermute | solution.py:219
  113.4 12.9 %collective-permute-done.22 = bf16[256,768]{1,0:T(8,128)(2,1)S(1)} collective-permute-done((bf16[256,768]{1,0:T(8,128)(2,1)S(1)}, bf16[256,768]{1,0:T(8,128)(2,1)S(1)}, u32[]{:S(2)}, u32[]{:S(2)}) %collective-permute-start.22) | collective-permute-done | bytes 393248 | tf_op jit(solution)/shard_map/u_near/ppermute | solution.py:219
  127.5 1.5 collective-permute-start.29
  129.4 2.6 %collective-permute-start.26 = (bf16[256,768]{1,0:T(8,128)(2,1)S(1)}, bf16[256,768]{1,0:T(8,128)(2,1)S(1)}, u32[]{:S(2)}, u32[]{:S(2)}) collective-permute-start(bf16[256,768]{1,0:T(8,128)(2,1)S(1)} %collective-permute-done.25), channel_id=1, source_target_pairs={{0,2},{2,0},{1,3},{3,1},{4,6},{6,4},{5,7},{7,5},{8,10},{10,8},{9,1... | collective-permute-start | bytes 1179656 | tf_op jit(solution)/shard_map/vert_f/ppermute | solution.py:219
  132.0 1.6 maximum_bitcast_fusion
  133.6 1.6 maximum_bitcast_fusion.1
  135.5 1.6 maximum_bitcast_fusion.2
  137.1 2.0 %collective-permute-done.29 = bf16[256,768]{1,0:T(8,128)(2,1)S(1)} collective-permute-done((bf16[256,768]{1,0:T(8,128)(2,1)S(1)}, bf16[256,768]{1,0:T(8,128)(2,1)S(1)}, u32[]{:S(2)}, u32[]{:S(2)}) %collective-permute-start.29) | collective-permute-done | bytes 393248 | tf_op jit(solution)/shard_map/hori_z/ppermute | solution.py:219
  139.1 2.9 %collective-permute-done.26 = bf16[256,768]{1,0:T(8,128)(2,1)S(1)} collective-permute-done((bf16[256,768]{1,0:T(8,128)(2,1)S(1)}, bf16[256,768]{1,0:T(8,128)(2,1)S(1)}, u32[]{:S(2)}, u32[]{:S(2)}) %collective-permute-start.26) | collective-permute-done | bytes 393248 | tf_op jit(solution)/shard_map/vert_f/ppermute | solution.py:219
  143.4 5.2 %collective-permute-done.24 = bf16[224,768]{1,0:T(8,128)(2,1)S(1)} collective-permute-done((bf16[224,768]{1,0:T(8,128)(2,1)S(1)}, bf16[224,768]{1,0:T(8,128)(2,1)S(1)}, u32[]{:S(2)}, u32[]{:S(2)}) %collective-permute-start.24) | collective-permute-done | bytes 344096 | tf_op jit(solution)/shard_map/u_grp_got/ppermute | solution.py:219
  148.8 2.9 %collective-permute-done.30 = bf16[256,768]{1,0:T(8,128)(2,1)S(1)} collective-permute-done((bf16[256,768]{1,0:T(8,128)(2,1)S(1)}, bf16[256,768]{1,0:T(8,128)(2,1)S(1)}, u32[]{:S(2)}, u32[]{:S(2)}) %collective-permute-start.30) | collective-permute-done | bytes 393248 | tf_op jit(solution)/shard_map/hori_f/ppermute | solution.py:219
  152.5 2.5 %collective-permute-start.28 = (bf16[112,768]{1,0:T(8,128)(2,1)S(1)}, bf16[112,768]{1,0:T(8,128)(2,1)S(1)}, u32[]{:S(2)}, u32[]{:S(2)}) collective-permute-start(bf16[112,768]{1,0:T(8,128)(2,1)S(1)} %split.85), channel_id=1, source_target_pairs={{0,16},{4,20},{8,24},{12,28},{16,0},{20,4},{24,8},{28,12},{1,17},{... | collective-permute-start | bytes 516104 | tf_op jit(solution)/shard_map/u_far_got/ppermute | solution.py:219
  156.4 7.4 %collective-permute-done.28 = bf16[112,768]{1,0:T(8,128)(2,1)S(1)} collective-permute-done((bf16[112,768]{1,0:T(8,128)(2,1)S(1)}, bf16[112,768]{1,0:T(8,128)(2,1)S(1)}, u32[]{:S(2)}, u32[]{:S(2)}) %collective-permute-start.28) | collective-permute-done | bytes 172064 | tf_op jit(solution)/shard_map/u_far_got/ppermute | solution.py:219
  164.1 1.8 collective-permute-start.33
  166.0 1.7 collective-permute-start.31
  167.8 4.5 %collective-permute-done.34 = bf16[112,768]{1,0:T(8,128)(2,1)S(1)} collective-permute-done((bf16[112,768]{1,0:T(8,128)(2,1)S(1)}, bf16[112,768]{1,0:T(8,128)(2,1)S(1)}, u32[]{:S(2)}, u32[]{:S(2)}) %collective-permute-start.34) | collective-permute-done | bytes 172064 | tf_op jit(solution)/shard_map/near_turned/ppermute | solution.py:219
  173.7 2.6 %convolution_convert_fusion.1 = bf16[112,1024]{1,0:T(8,128)(2,1)S(1)} fusion(bf16[112,768]{1,0:T(8,128)(2,1)S(1)} %collective-permute-done.34, bf16[112,768]{1,0:T(8,128)(2,1)} %collective-permute-done.33, bf16[512,1536]{1,0:T(8,128)(2,1)} %collective-permute-done.32, bf16[256,768]{1,0:T(8,128)(2,1)} %copy-done.24, ...), kind=kOutput, calls=%fused_computation.18 | convolution fusion | flops 368852992 | bytes 3719168 | tf_op jit(solution)/shard_map/dot_general | solution.py:323
  176.9 2.8 %convolution_convert_fusion.2 = bf16[112,1024]{1,0:T(8,128)(2,1)S(1)} fusion(bf16[112,768]{1,0:T(8,128)(2,1)S(1)} %collective-permute-done.31, bf16[112,768]{1,0:T(8,128)(2,1)} %copy-done.28, bf16[512,1536]{1,0:T(8,128)(2,1)} %collective-permute-done.32, bf16[256,768]{1,0:T(8,128)(2,1)S(1)} %copy-done.25, bf16[256,768]{1,0:T(8,128)(2,1)S(1)} %get-tuple-element.196, ...), kind=kOutput, calls=%fused_computation.19 | convolution fusion | flops 368852992 | bytes 3719168 | tf_op jit(solution)/shard_map/dot_general | solution.py:323
  179.7 3.2 %collective-permute-done.35 = bf16[112,1024]{1,0:T(8,128)(2,1)S(1)} collective-permute-done((bf16[112,1024]{1,0:T(8,128)(2,1)S(1)}, bf16[112,1024]{1,0:T(8,128)(2,1)S(1)}, u32[]{:S(2)}, u32[]{:S(2)}) %collective-permute-start.35) | collective-permute-done | bytes 229408 | tf_op jit(solution)/shard_map/near_out_got/ppermute | solution.py:219
  182.9 3.1 %shard_map.139 = bf16[512,2048]{1,0:T(8,128)(2,1)} custom-call(s32[2]{0:T(128)S(1)} %copy-done.14, bf16[512,112]{1,0:T(8,128)(2,1)S(1)} %copy-done.8, f32[512,1]{1,0:T(8,128)S(1)} %copy.20.weight, bf16[112,2048]{1,0:T(8,128)(2,1)S(1)} %pad_maximum_fusion.4.values), custom_call_target="tpu_custom_call" | custom-call | tf_op jit(solution)/shard_map/pallas_call | solution.py:152
  (153 shorter events, 22.6 us)
Async XLA Ops:
  0.6 12.5 %copy-start = (bf16[512,2048]{1,0:T(8,128)(2,1)S(1)}, bf16[512,2048]{1,0:T(8,128)(2,1)}, u32[]{:S(2)}) copy-start(bf16[512,2048]{1,0:T(8,128)(2,1)} %param.17) | copy-start | bytes 6291460
  3.6 7.1 %collective-permute-start.1 = (bf16[344,1024]{1,0:T(8,128)(2,1)}, bf16[344,1024]{1,0:T(8,128)(2,1)}, u32[]{:S(2)}, u32[]{:S(2)}) collective-permute-start(bf16[344,1024]{1,0:T(8,128)(2,1)} %shard_map.130), channel_id=1, source_target_pairs={{0,4},{4,0},{8,12},{12,8},{16,20},{20,16},{24,28},{28,24},{1,5},{5... | collective-permute-start | bytes 2113544 | tf_op jit(solution)/shard_map/cot_got/ppermute | solution.py:219
  7.4 3.3 %collective-permute-start = (bf16[344,768]{1,0:T(8,128)(2,1)}, bf16[344,768]{1,0:T(8,128)(2,1)}, u32[]{:S(2)}, u32[]{:S(2)}) collective-permute-start(bf16[344,768]{1,0:T(8,128)(2,1)} %get-tuple-element.87.refs_0_), channel_id=1, source_target_pairs={{0,4},{4,0},{8,12},{12,8},{16,20},{20,16},{24,28},{28,24},{1,5},{5... | collective-permute-start | bytes 1585160 | tf_op jit(solution)/shard_map/act_got/ppermute | solution.py:219
  14.2 3.6 %collective-permute-start.3 = (bf16[344,1024]{1,0:T(8,128)(2,1)S(1)}, bf16[344,1024]{1,0:T(8,128)(2,1)S(1)}, u32[]{:S(2)}, u32[]{:S(2)}) collective-permute-start(bf16[344,1024]{1,0:T(8,128)(2,1)S(1)} %copy-done.21), channel_id=1, source_target_pairs={{0,4},{4,0},{8,12},{12,8},{16,20},{20,16},{24,28},{28,24},{1,5},{5... | collective-permute-start | bytes 2113544 | tf_op jit(solution)/shard_map/in_got/ppermute | solution.py:219
  14.7 3.1 %collective-permute-start.2 = (bf16[344,768]{1,0:T(8,128)(2,1)S(1)}, bf16[344,768]{1,0:T(8,128)(2,1)S(1)}, u32[]{:S(2)}, u32[]{:S(2)}) collective-permute-start(bf16[344,768]{1,0:T(8,128)(2,1)S(1)} %copy-done.6), channel_id=1, source_target_pairs={{0,4},{4,0},{8,12},{12,8},{16,20},{20,16},{24,28},{28,24},{1,5},{5... | collective-permute-start | bytes 1585160 | tf_op jit(solution)/shard_map/gate_got/ppermute | solution.py:219
  14.9 18.6 %collective-permute-start.6 = (bf16[256,768]{1,0:T(8,128)(2,1)S(1)}, bf16[256,768]{1,0:T(8,128)(2,1)S(1)}, u32[]{:S(2)}, u32[]{:S(2)}) collective-permute-start(bf16[256,768]{1,0:T(8,128)(2,1)S(1)} %shard_map.131), channel_id=1, source_target_pairs={{0,8},{4,12},{8,0},{12,4},{16,24},{20,28},{24,16},{28,20},{1,9},{5... | collective-permute-start | bytes 1179656 | tf_op jit(solution)/shard_map/d_b/ppermute | solution.py:219
  19.4 21.7 %collective-permute-start.5 = (bf16[256,768]{1,0:T(8,128)(2,1)S(1)}, bf16[256,768]{1,0:T(8,128)(2,1)S(1)}, u32[]{:S(2)}, u32[]{:S(2)}) collective-permute-start(bf16[256,768]{1,0:T(8,128)(2,1)S(1)} %get-tuple-element.100), channel_id=1, source_target_pairs={{0,8},{4,12},{8,0},{12,4},{16,24},{20,28},{24,16},{28,20},{1,9},{5... | collective-permute-start | bytes 1179656 | tf_op jit(solution)/shard_map/g_b/ppermute | solution.py:219
  21.8 22.3 %collective-permute-start.10 = (bf16[112,1024]{1,0:T(8,128)(2,1)S(1)}, bf16[112,1024]{1,0:T(8,128)(2,1)S(1)}, u32[]{:S(2)}, u32[]{:S(2)}) collective-permute-start(bf16[112,1024]{1,0:T(8,128)(2,1)S(1)} %constant_dynamic-slice_fusion), channel_id=1, source_target_pairs={{0,16},{4,20},{8,24},{12,28},{16,0},{20,4},{24,8},{28,12},{1,17},{... | collective-permute-start | bytes 688136 | tf_op jit(solution)/shard_map/there/ppermute | solution.py:219
  24.4 23.0 %collective-permute-start.12 = (bf16[344,768]{1,0:T(8,128)(2,1)S(1)}, bf16[344,768]{1,0:T(8,128)(2,1)}, u32[]{:S(2)}, u32[]{:S(2)}) collective-permute-start(bf16[344,768]{1,0:T(8,128)(2,1)S(1)} %copy-done.5), channel_id=1, source_target_pairs={{0,4},{4,0},{8,12},{12,8},{16,20},{20,16},{24,28},{28,24},{1,5},{5... | collective-permute-start | bytes 1585160 | tf_op jit(solution)/shard_map/up_got/ppermute | solution.py:219
  31.0 48.6 %collective-permute-start.8 = (bf16[256,768]{1,0:T(8,128)(2,1)}, bf16[256,768]{1,0:T(8,128)(2,1)}, u32[]{:S(2)}, u32[]{:S(2)}) collective-permute-start(bf16[256,768]{1,0:T(8,128)(2,1)} %get-tuple-element.101), channel_id=1, source_target_pairs={{0,8},{4,12},{8,0},{12,4},{16,24},{20,28},{24,16},{28,20},{1,9},{5... | collective-permute-start | bytes 1179656 | tf_op jit(solution)/shard_map/d_a/ppermute | solution.py:219
  33.5 13.9 %copy-start.14 = (s32[2]{0:T(128)S(1)}, s32[2]{0:T(128)}, u32[]{:S(2)}) copy-start(s32[2]{0:T(128)} %pad_add_fusion.place_ref) | copy-start | bytes 28
  33.6 40.3 %collective-permute-start.4 = (bf16[256,768]{1,0:T(8,128)(2,1)}, bf16[256,768]{1,0:T(8,128)(2,1)}, u32[]{:S(2)}, u32[]{:S(2)}) collective-permute-start(bf16[256,768]{1,0:T(8,128)(2,1)} %get-tuple-element.104), channel_id=1, source_target_pairs={{0,8},{4,12},{8,0},{12,4},{16,24},{20,28},{24,16},{28,20},{1,9},{5... | collective-permute-start | bytes 1179656 | tf_op jit(solution)/shard_map/g_a/ppermute | solution.py:219
  41.1 33.4 %collective-permute-start.9 = (bf16[256,768]{1,0:T(8,128)(2,1)}, bf16[256,768]{1,0:T(8,128)(2,1)}, u32[]{:S(2)}, u32[]{:S(2)}) collective-permute-start(bf16[256,768]{1,0:T(8,128)(2,1)} %add_convert_fusion.1), channel_id=1, source_target_pairs={{0,16},{4,20},{8,24},{12,28},{16,0},{20,4},{24,8},{28,12},{1,17},{... | collective-permute-start | bytes 1179656 | tf_op jit(solution)/shard_map/d_across/ppermute | solution.py:219
  44.8 34.8 %collective-permute-start.7 = (bf16[256,768]{1,0:T(8,128)(2,1)}, bf16[256,768]{1,0:T(8,128)(2,1)}, u32[]{:S(2)}, u32[]{:S(2)}) collective-permute-start(bf16[256,768]{1,0:T(8,128)(2,1)} %add_convert_fusion.2), channel_id=1, source_target_pairs={{0,16},{4,20},{8,24},{12,28},{16,0},{20,4},{24,8},{28,12},{1,17},{... | collective-permute-start | bytes 1179656 | tf_op jit(solution)/shard_map/g_across/ppermute | solution.py:219
  47.4 5.9 %collective-permute-start.11 = (bf16[2,112,512]{2,1,0:T(8,128)(2,1)}, bf16[2,112,512]{2,1,0:T(8,128)(2,1)}, u32[]{:S(2)}, u32[]{:S(2)}) collective-permute-start(bf16[2,112,512]{2,1,0:T(8,128)(2,1)} %get-tuple-element.112), channel_id=1, source_target_pairs={{0,4},{4,0},{8,12},{12,8},{16,20},{20,16},{24,28},{28,24},{1,5},{5... | collective-permute-start | bytes 688136 | tf_op jit(solution)/shard_map/row_got/ppermute | solution.py:219
  47.5 32.1 %copy-start.19 = (f32[1,256,3,768]{3,1,2,0:T(8,128)S(1)}, f32[1,256,3,768]{3,1,2,0:T(8,128)}, u32[]{:S(2)}) copy-start(f32[1,256,3,768]{3,1,2,0:T(8,128)} %param.15) | copy-start | bytes 7077892
  47.5 32.1 %copy-start.20 = (f32[1,256,3,768]{3,1,2,0:T(8,128)S(1)}, f32[1,256,3,768]{3,1,2,0:T(8,128)}, u32[]{:S(2)}) copy-start(f32[1,256,3,768]{3,1,2,0:T(8,128)} %param.16) | copy-start | bytes 7077892
  50.4 29.2 %copy-start.10 = (f32[256,768]{1,0:T(8,128)S(1)}, f32[256,768]{1,0:T(8,128)}, u32[]{:S(2)}) copy-start(f32[256,768]{1,0:T(8,128)} %copy-done.9) | copy-start | bytes 2359300
  50.4 29.2 %copy-start.12 = (f32[256,768]{1,0:T(8,128)S(1)}, f32[256,768]{1,0:T(8,128)}, u32[]{:S(2)}) copy-start(f32[256,768]{1,0:T(8,128)} %copy-done.11) | copy-start | bytes 2359300
  50.4 29.2 %copy-start.18 = (f32[1,256,3,768]{3,1,2,0:T(8,128)S(1)}, f32[1,256,3,768]{3,1,2,0:T(8,128)}, u32[]{:S(2)}) copy-start(f32[1,256,3,768]{3,1,2,0:T(8,128)} %param.14) | copy-start | bytes 7077892
  53.4 29.5 %collective-permute-start.13 = (bf16[256,768]{1,0:T(8,128)(2,1)S(1)}, bf16[256,768]{1,0:T(8,128)(2,1)S(1)}, u32[]{:S(2)}, u32[]{:S(2)}) collective-permute-start(bf16[256,768]{1,0:T(8,128)(2,1)S(1)} %get-tuple-element.116), channel_id=1, source_target_pairs={{0,8},{4,12},{8,0},{12,4},{16,24},{20,28},{24,16},{28,20},{1,9},{5... | collective-permute-start | bytes 1179656 | tf_op jit(solution)/shard_map/u_b/ppermute | solution.py:219
  73.8 12.7 %collective-permute-start.16 = (bf16[2,2,112,512]{3,2,1,0:T(8,128)(2,1)S(1)}, bf16[2,2,112,512]{3,2,1,0:T(8,128)(2,1)S(1)}, u32[]{:S(2)}, u32[]{:S(2)}) collective-permute-start(bf16[2,2,112,512]{3,2,1,0:T(8,128)(2,1)S(1)} %pad_maximum_fusion.3), channel_id=1, source_target_pairs={{0,0},{1,2},{2,1},{3,3},{4,4},{5,6},{6,5},{7,7},{8,8},{9,10},{10,9... | collective-permute-start | bytes 1376264 | tf_op jit(solution)/shard_map/turned/ppermute | solution.py:219
  74.5 16.5 %collective-permute-start.17 = (bf16[2,2,112,512]{3,2,1,0:T(8,128)(2,1)S(1)}, bf16[2,2,112,512]{3,2,1,0:T(8,128)(2,1)S(1)}, u32[]{:S(2)}, u32[]{:S(2)}) collective-permute-start(bf16[2,2,112,512]{3,2,1,0:T(8,128)(2,1)S(1)} %pad_maximum_fusion.3), channel_id=1, source_target_pairs={{0,1},{1,3},{3,2},{2,0},{4,5},{5,7},{7,6},{6,4},{8,9},{9,11},{11,1... | collective-permute-start | bytes 1376264 | tf_op jit(solution)/shard_map/rotated/ppermute | solution.py:219
  82.4 14.5 %collective-permute-start.18 = (bf16[256,768]{1,0:T(8,128)(2,1)S(1)}, bf16[256,768]{1,0:T(8,128)(2,1)S(1)}, u32[]{:S(2)}, u32[]{:S(2)}) collective-permute-start(bf16[256,768]{1,0:T(8,128)(2,1)S(1)} %get-tuple-element.160), channel_id=1, source_target_pairs={{0,2},{2,0},{1,3},{3,1},{4,6},{6,4},{5,7},{7,5},{8,10},{10,8},{9,1... | collective-permute-start | bytes 1179656 | tf_op jit(solution)/shard_map/vert_z/ppermute | solution.py:219
  82.5 20.5 %collective-permute-start.19 = (bf16[256,768]{1,0:T(8,128)(2,1)S(1)}, bf16[256,768]{1,0:T(8,128)(2,1)S(1)}, u32[]{:S(2)}, u32[]{:S(2)}) collective-permute-start(bf16[256,768]{1,0:T(8,128)(2,1)S(1)} %get-tuple-element.123), channel_id=1, source_target_pairs={{0,8},{4,12},{8,0},{12,4},{16,24},{20,28},{24,16},{28,20},{1,9},{5... | collective-permute-start | bytes 1179656 | tf_op jit(solution)/shard_map/g_near/ppermute | solution.py:219
  83.0 20.8 %collective-permute-start.15 = (bf16[256,768]{1,0:T(8,128)(2,1)S(1)}, bf16[256,768]{1,0:T(8,128)(2,1)S(1)}, u32[]{:S(2)}, u32[]{:S(2)}) collective-permute-start(bf16[256,768]{1,0:T(8,128)(2,1)S(1)} %add_convert_fusion), channel_id=1, source_target_pairs={{0,16},{4,20},{8,24},{12,28},{16,0},{20,4},{24,8},{28,12},{1,17},{... | collective-permute-start | bytes 1179656 | tf_op jit(solution)/shard_map/u_across/ppermute | solution.py:219
  86.5 21.9 %collective-permute-start.14 = (bf16[256,768]{1,0:T(8,128)(2,1)S(1)}, bf16[256,768]{1,0:T(8,128)(2,1)S(1)}, u32[]{:S(2)}, u32[]{:S(2)}) collective-permute-start(bf16[256,768]{1,0:T(8,128)(2,1)S(1)} %get-tuple-element.126), channel_id=1, source_target_pairs={{0,8},{4,12},{8,0},{12,4},{16,24},{20,28},{24,16},{28,20},{1,9},{5... | collective-permute-start | bytes 1179656 | tf_op jit(solution)/shard_map/u_a/ppermute | solution.py:219
  103.7 5.4 %collective-permute-start.20 = (bf16[448,768]{1,0:T(8,128)(2,1)S(1)}, bf16[448,768]{1,0:T(8,128)(2,1)S(1)}, u32[]{:S(2)}, u32[]{:S(2)}) collective-permute-start(bf16[448,768]{1,0:T(8,128)(2,1)S(1)} %split.81), channel_id=1, source_target_pairs={{0,4},{4,0},{8,12},{12,8},{16,20},{20,16},{24,28},{28,24},{1,5},{5... | collective-permute-start | bytes 2064392 | tf_op jit(solution)/shard_map/g_core_got/ppermute | solution.py:219
  109.4 17.4 %copy-start.16 = (f32[448,768]{1,0:T(8,128)}, f32[448,768]{1,0:T(8,128)S(1)}, u32[]{:S(2)}) copy-start(f32[448,768]{1,0:T(8,128)S(1)} %convert_add_fusion.1) | copy-start | bytes 4128772
  109.4 16.9 %collective-permute-start.22 = (bf16[256,768]{1,0:T(8,128)(2,1)S(1)}, bf16[256,768]{1,0:T(8,128)(2,1)S(1)}, u32[]{:S(2)}, u32[]{:S(2)}) collective-permute-start(bf16[256,768]{1,0:T(8,128)(2,1)S(1)} %get-tuple-element.148), channel_id=1, source_target_pairs={{0,8},{4,12},{8,0},{12,4},{16,24},{20,28},{24,16},{28,20},{1,9},{5... | collective-permute-start | bytes 1179656 | tf_op jit(solution)/shard_map/u_near/ppermute | solution.py:219
  110.9 18.4 %collective-permute-start.25 = (bf16[256,768]{1,0:T(8,128)(2,1)S(1)}, bf16[256,768]{1,0:T(8,128)(2,1)S(1)}, u32[]{:S(2)}, u32[]{:S(2)}) collective-permute-start(bf16[256,768]{1,0:T(8,128)(2,1)S(1)} %get-tuple-element.160), channel_id=1, source_target_pairs={{0,16},{4,20},{8,24},{12,28},{16,0},{20,4},{24,8},{28,12},{1,17},{... | collective-permute-start | bytes 1179656 | tf_op jit(solution)/shard_map/d_other/ppermute | solution.py:219
  127.4 7.8 %collective-permute-start.23 = (bf16[448,768]{1,0:T(8,128)(2,1)S(1)}, bf16[448,768]{1,0:T(8,128)(2,1)S(1)}, u32[]{:S(2)}, u32[]{:S(2)}) collective-permute-start(bf16[448,768]{1,0:T(8,128)(2,1)S(1)} %split.80), channel_id=1, source_target_pairs={{0,4},{4,0},{8,12},{12,8},{16,20},{20,16},{24,28},{28,24},{1,5},{5... | collective-permute-start | bytes 2064392 | tf_op jit(solution)/shard_map/u_core_got/ppermute | solution.py:219
  127.5 11.5 %collective-permute-start.29 = (bf16[256,768]{1,0:T(8,128)(2,1)S(1)}, bf16[256,768]{1,0:T(8,128)(2,1)S(1)}, u32[]{:S(2)}, u32[]{:S(2)}) collective-permute-start(bf16[256,768]{1,0:T(8,128)(2,1)S(1)} %broadcast_select_fusion.5), channel_id=1, source_target_pairs={{0,1},{1,0},{2,3},{3,2},{4,5},{5,4},{6,7},{7,6},{8,9},{9,8},{10,11... | collective-permute-start | bytes 1179656 | tf_op jit(solution)/shard_map/hori_z/ppermute | solution.py:219
  129.1 19.6 %collective-permute-start.21 = (bf16[224,768]{1,0:T(8,128)(2,1)S(1)}, bf16[224,768]{1,0:T(8,128)(2,1)S(1)}, u32[]{:S(2)}, u32[]{:S(2)}) collective-permute-start(bf16[224,768]{1,0:T(8,128)(2,1)S(1)} %split.83), channel_id=1, source_target_pairs={{0,16},{4,20},{8,24},{12,28},{16,0},{20,4},{24,8},{28,12},{1,17},{... | collective-permute-start | bytes 1032200 | tf_op jit(solution)/shard_map/g_far_got/ppermute | solution.py:219
  129.4 12.6 %collective-permute-start.26 = (bf16[256,768]{1,0:T(8,128)(2,1)S(1)}, bf16[256,768]{1,0:T(8,128)(2,1)S(1)}, u32[]{:S(2)}, u32[]{:S(2)}) collective-permute-start(bf16[256,768]{1,0:T(8,128)(2,1)S(1)} %collective-permute-done.25), channel_id=1, source_target_pairs={{0,2},{2,0},{1,3},{3,1},{4,6},{6,4},{5,7},{7,5},{8,10},{10,8},{9,1... | collective-permute-start | bytes 1179656 | tf_op jit(solution)/shard_map/vert_f/ppermute | solution.py:219
  135.4 13.1 %collective-permute-start.24 = (bf16[224,768]{1,0:T(8,128)(2,1)S(1)}, bf16[224,768]{1,0:T(8,128)(2,1)S(1)}, u32[]{:S(2)}, u32[]{:S(2)}) collective-permute-start(bf16[224,768]{1,0:T(8,128)(2,1)S(1)} %split.82), channel_id=1, source_target_pairs={{0,2},{2,0},{1,3},{3,1},{4,6},{6,4},{5,7},{7,5},{8,10},{10,8},{9,1... | collective-permute-start | bytes 1032200 | tf_op jit(solution)/shard_map/u_grp_got/ppermute | solution.py:219
  137.1 11.6 %slice-start = ((f32[448,768]{1,0:T(8,128)}), f32[224,768]{1,0:T(8,128)S(1)}, s32[]{:S(2)}) async-start(f32[448,768]{1,0:T(8,128)} %copy-done.16), calls=%async_computation | async-start | bytes 1376256 | tf_op jit(solution)/shard_map/split | solution.py:312
  139.0 34.7 %copy-start.23 = (bf16[256,768]{1,0:T(8,128)(2,1)}, bf16[256,768]{1,0:T(8,128)(2,1)S(1)}, u32[]{:S(2)}) copy-start(bf16[256,768]{1,0:T(8,128)(2,1)S(1)} %collective-permute-done.29) | copy-start | bytes 1179652
  142.1 9.6 %collective-permute-start.30 = (bf16[256,768]{1,0:T(8,128)(2,1)S(1)}, bf16[256,768]{1,0:T(8,128)(2,1)S(1)}, u32[]{:S(2)}, u32[]{:S(2)}) collective-permute-start(bf16[256,768]{1,0:T(8,128)(2,1)S(1)} %broadcast_select_fusion.4), channel_id=1, source_target_pairs={{0,1},{1,0},{2,3},{3,2},{4,5},{5,4},{6,7},{7,6},{8,9},{9,8},{10,11... | collective-permute-start | bytes 1179656 | tf_op jit(solution)/shard_map/hori_f/ppermute | solution.py:219
  152.4 21.3 %collective-permute-start.32 = (bf16[512,1536]{1,0:T(8,128)(2,1)S(1)}, bf16[512,1536]{1,0:T(8,128)(2,1)}, u32[]{:S(2)}, u32[]{:S(2)}) collective-permute-start(bf16[512,1536]{1,0:T(8,128)(2,1)S(1)} %maximum_maximum_fusion), channel_id=1, source_target_pairs={{0,4},{4,0},{8,12},{12,8},{16,20},{20,16},{24,28},{28,24},{1,5},{5... | collective-permute-start | bytes 4718600 | tf_op jit(solution)/shard_map/down_got/ppermute | solution.py:219
  152.5 11.4 %collective-permute-start.28 = (bf16[112,768]{1,0:T(8,128)(2,1)S(1)}, bf16[112,768]{1,0:T(8,128)(2,1)S(1)}, u32[]{:S(2)}, u32[]{:S(2)}) collective-permute-start(bf16[112,768]{1,0:T(8,128)(2,1)S(1)} %split.85), channel_id=1, source_target_pairs={{0,16},{4,20},{8,24},{12,28},{16,0},{20,4},{24,8},{28,12},{1,17},{... | collective-permute-start | bytes 516104 | tf_op jit(solution)/shard_map/u_far_got/ppermute | solution.py:219
  155.0 8.9 %collective-permute-start.27 = (bf16[112,768]{1,0:T(8,128)(2,1)S(1)}, bf16[112,768]{1,0:T(8,128)(2,1)S(1)}, u32[]{:S(2)}, u32[]{:S(2)}) collective-permute-start(bf16[112,768]{1,0:T(8,128)(2,1)S(1)} %split.84), channel_id=1, source_target_pairs={{0,2},{2,0},{1,3},{3,1},{4,6},{6,4},{5,7},{7,5},{8,10},{10,8},{9,1... | collective-permute-start | bytes 516104 | tf_op jit(solution)/shard_map/g_grp_got/ppermute | solution.py:219
  164.0 12.4 %copy-start.28 = (bf16[112,768]{1,0:T(8,128)(2,1)}, bf16[112,768]{1,0:T(8,128)(2,1)S(1)}, u32[]{:S(2)}) copy-start(bf16[112,768]{1,0:T(8,128)(2,1)S(1)} %fusion.25) | copy-start | bytes 516100
  164.0 8.3 %collective-permute-start.34 = (bf16[112,768]{1,0:T(8,128)(2,1)S(1)}, bf16[112,768]{1,0:T(8,128)(2,1)S(1)}, u32[]{:S(2)}, u32[]{:S(2)}) collective-permute-start(bf16[112,768]{1,0:T(8,128)(2,1)S(1)} %fusion.25), channel_id=1, source_target_pairs={{0,9},{1,8},{4,13},{5,12},{8,1},{9,0},{12,5},{13,4},{16,25},{17,24... | collective-permute-start | bytes 516104 | tf_op jit(solution)/shard_map/near_turned/ppermute | solution.py:219
  164.1 9.6 %collective-permute-start.33 = (bf16[112,768]{1,0:T(8,128)(2,1)S(1)}, bf16[112,768]{1,0:T(8,128)(2,1)}, u32[]{:S(2)}, u32[]{:S(2)}) collective-permute-start(bf16[112,768]{1,0:T(8,128)(2,1)S(1)} %fusion.25), channel_id=1, source_target_pairs={{0,8},{4,12},{8,0},{12,4},{16,24},{20,28},{24,16},{28,20},{1,9},{5... | collective-permute-start | bytes 516104 | tf_op jit(solution)/shard_map/near_hidden/ppermute | solution.py:219
  166.0 10.9 %copy-start.25 = (bf16[256,768]{1,0:T(8,128)(2,1)S(1)}, bf16[256,768]{1,0:T(8,128)(2,1)}, u32[]{:S(2)}) copy-start(bf16[256,768]{1,0:T(8,128)(2,1)} %copy-done.24) | copy-start | bytes 1179652
  166.0 10.9 %collective-permute-start.31 = (bf16[112,768]{1,0:T(8,128)(2,1)S(1)}, bf16[112,768]{1,0:T(8,128)(2,1)S(1)}, u32[]{:S(2)}, u32[]{:S(2)}) collective-permute-start(bf16[112,768]{1,0:T(8,128)(2,1)S(1)} %fusion.25), channel_id=1, source_target_pairs={{0,1},{1,0},{2,3},{3,2},{4,5},{5,4},{6,7},{7,6},{8,9},{9,8},{10,11... | collective-permute-start | bytes 516104 | tf_op jit(solution)/shard_map/beside/ppermute | solution.py:219
  176.4 6.5 %collective-permute-start.35 = (bf16[112,1024]{1,0:T(8,128)(2,1)S(1)}, bf16[112,1024]{1,0:T(8,128)(2,1)S(1)}, u32[]{:S(2)}, u32[]{:S(2)}) collective-permute-start(bf16[112,1024]{1,0:T(8,128)(2,1)S(1)} %convolution_convert_fusion.1), channel_id=1, source_target_pairs={{0,8},{4,12},{8,0},{12,4},{16,24},{20,28},{24,16},{28,20},{1,9},{5... | collective-permute-start | bytes 688136 | tf_op jit(solution)/shard_map/near_out_got/ppermute | solution.py:219
  (20 other events, 80.1 us)

commit v2 on v1

--- a/solution.py
+++ b/solution.py
@@ -148,13 +148,13 @@
 
 def spread(values, slots, weight, place):
     count, width = slots.shape[0], values.shape[1]
-    step = count // 4
+    step = count // 2
     return pl.pallas_call(
         spread_kernel,
         out_shape=jax.ShapeDtypeStruct((count, width), BF16),
         grid_spec=pltpu.PrefetchScalarGridSpec(
             num_scalar_prefetch=1,
-            grid=(4,),
+            grid=(2,),
             in_specs=[
                 pl.BlockSpec((step, CAP), lambda i, p: (i, 0)),
                 pl.BlockSpec((step, 1), lambda i, p: (i, 0)),
@@ -382,9 +382,9 @@
     u_grp, u_quarter = step(folded, u_half, u_core_got)
     u_grp_got = send("u_grp_got", u_grp, "grp", SWAP)
     relay_f = step(relayed, d_other, vert_f)
-    hori_f = send("hori_f", relay_f, "tp", SWAP)
     u_far, u_sum = step(folded, u_quarter, u_grp_got)
     u_far_got = send("u_far_got", u_far, "fsdp", FAR)
+    hori_f = send("hori_f", relay_f, "tp", SWAP)
     g_grp, g_sum = step(folded, g_quarter, g_far_got)
     g_grp_got = send("g_grp_got", g_grp, "grp", SWAP)
     down = step(plane_weights, d_shard, vert_z, hori_z, d_other, vert_f, hori_f)

time: 186 us -> 186 us (level)
  no operation moved by 1% of the time
where the time goes in v2:
time: 186 us; the launch traced here: 185 us
  waiting for transfers between devices  83.9 us (45%)
  starting transfers between devices  45.1 us (24%)
  Pallas kernels  26.6 us (14%)
  other arithmetic  15.2 us (8%)
  matrix products  8.01 us (4%)
  local copies, waits for them, and re-layouts  5.26 us (3%)
    ppermute x36, waiting for transfers between devices, send(): return lax.ppermute(block, axis, pairs)  83.9 us
    ppermute x36, starting transfers between devices, send(): return lax.ppermute(block, axis, pairs)  45.1 us
    pallas_call x7, Pallas kernels, token_products(): pl.pallas_call(product_kernel, out_shape=outs, grid_spec=pltpu.PrefetchSc...  17.5 us
    dot_general x2, matrix products, down_product(): lax.dot_general(slots, down, BY_LAST, preferred_element_type=F32)  5.44 us
    broadcast_in_dim x3, other arithmetic, stacked(): return tuple((jnp.stack(news[i::3], axis=1)[None] for i in range(3)))  4.67 us
    pallas_call x2, Pallas kernels, take_columns(): pl.pallas_call(functools.partial(take_kernel, rows, order), out_shape=(ha...  4.65 us
  transfers between devices with their start and end apart: 36, of which 15 were waited for; matrix products, arithmetic and copies ran while one was open for 13% of the time, Pallas kernels for 10%

profile of v2, /device:TPU:0, one launch (start us, length us, event | category | flops | bytes accessed | tf_op | source)
XLA Modules:
  0.0 185.4 jit_solution(6780150709685775329)
XLA Ops:
  1.3 2.3 %shard_map.130 = bf16[344,1024]{1,0:T(8,128)(2,1)} custom-call(s32[2]{0:T(128)} %pad_add_fusion.place_ref, bf16[344,2048]{1,0:T(8,128)(2,1)} %refs_3_.6), custom_call_target="tpu_custom_call" | custom-call | tf_op jit(solution)/shard_map/pallas_call | solution.py:87
  4.0 1.5 fusion.46
  5.6 1.8 fusion.3
  7.5 2.3 %shard_map.129 = bf16[344,1024]{1,0:T(8,128)(2,1)} custom-call(s32[2]{0:T(128)} %pad_add_fusion.place_ref, bf16[344,2048]{1,0:T(8,128)(2,1)} %refs_3_.9), custom_call_target="tpu_custom_call" | custom-call | tf_op jit(solution)/shard_map/pallas_call | solution.py:87
  10.7 2.4 %shard_map.131 = bf16[256,768]{1,0:T(8,128)(2,1)S(1)} custom-call(s32[2]{0:T(128)S(1)} %copy-done.13, bf16[344,768]{1,0:T(8,128)(2,1)} %get-tuple-element.87.refs_0_, bf16[344,768]{1,0:T(8,128)(2,1)} %collective-permute-done.refs_1_, bf16[344,2048]{1,0:T(8,128)(2,1)S(1)} %copy-done.3, bf16[344,1024]{1,0:T(8,128)(2,1)} %collective-permute-done.1.refs_3_.refs_4_.refs_5_), custom_call_target="tpu_custom_call" | custom-call | tf_op jit(solution)/shard_map/pallas_call | solution.py:123
  14.9 2.9 %collective-permute-start.6 = (bf16[256,768]{1,0:T(8,128)(2,1)S(1)}, bf16[256,768]{1,0:T(8,128)(2,1)S(1)}, u32[]{:S(2)}, u32[]{:S(2)}) collective-permute-start(bf16[256,768]{1,0:T(8,128)(2,1)S(1)} %shard_map.131), channel_id=1, source_target_pairs={{0,8},{4,12},{8,0},{12,4},{16,24},{20,28},{24,16},{28,20},{1,9},{5... | collective-permute-start | bytes 1179656 | tf_op jit(solution)/shard_map/d_b/ppermute | solution.py:219
  17.8 1.6 shard_map.135
  19.4 2.4 %collective-permute-start.5 = (bf16[256,768]{1,0:T(8,128)(2,1)S(1)}, bf16[256,768]{1,0:T(8,128)(2,1)S(1)}, u32[]{:S(2)}, u32[]{:S(2)}) collective-permute-start(bf16[256,768]{1,0:T(8,128)(2,1)S(1)} %get-tuple-element.100), channel_id=1, source_target_pairs={{0,8},{4,12},{8,0},{12,4},{16,24},{20,28},{24,16},{28,20},{1,9},{5... | collective-permute-start | bytes 1179656 | tf_op jit(solution)/shard_map/g_b/ppermute | solution.py:219
  21.8 2.6 %collective-permute-start.10 = (bf16[112,1024]{1,0:T(8,128)(2,1)S(1)}, bf16[112,1024]{1,0:T(8,128)(2,1)S(1)}, u32[]{:S(2)}, u32[]{:S(2)}) collective-permute-start(bf16[112,1024]{1,0:T(8,128)(2,1)S(1)} %constant_dynamic-slice_fusion), channel_id=1, source_target_pairs={{0,16},{4,20},{8,24},{12,28},{16,0},{20,4},{24,8},{28,12},{1,17},{... | collective-permute-start | bytes 688136 | tf_op jit(solution)/shard_map/there/ppermute | solution.py:219
  24.4 2.4 %shard_map.133 = f32[256,768]{1,0:T(8,128)S(1)} custom-call(s32[2]{0:T(128)S(1)} %copy-done.13, bf16[344,768]{1,0:T(8,128)(2,1)} %get-tuple-element.87.refs_0_, bf16[344,768]{1,0:T(8,128)(2,1)} %collective-permute-done.refs_1_, bf16[344,2048]{1,0:T(8,128)(2,1)S(1)} %copy-done.4, bf16[344,1024]{1,0:T(8,128)(2,1)} %collective-permute-done.1.refs_3_.refs_4_.refs_5_), custom_call_target="tpu_custom_call" | custom-call | tf_op jit(solution)/shard_map/pallas_call | solution.py:123
  26.8 3.3 %shard_map.134 = (bf16[256,768]{1,0:T(8,128)(2,1)}, f32[256,768]{1,0:T(8,128)S(1)}) custom-call(s32[2]{0:T(128)S(1)} %copy-done.13, bf16[344,768]{1,0:T(8,128)(2,1)} %get-tuple-element.87.refs_0_, bf16[344,768]{1,0:T(8,128)(2,1)} %collective-permute-done.refs_1_, bf16[344,2048]{1,0:T(8,128)(2,1)S(1)} %copy-done.4, bf16[344,2048]{1,0:T(8,128)(2,1)S(1)} %copy-done.4, ...), custom_call_target="tpu_custom_call" | custom-call | tf_op jit(solution)/shard_map/pallas_call | solution.py:123
  31.5 2.0 %shard_map.132 = (bf16[256,768]{1,0:T(8,128)(2,1)}, f32[256,768]{1,0:T(8,128)S(1)}) custom-call(s32[2]{0:T(128)S(1)} %copy-done.13, bf16[344,768]{1,0:T(8,128)(2,1)S(1)} %copy-done.6, bf16[344,768]{1,0:T(8,128)(2,1)S(1)} %collective-permute-done.2.refs_1_, bf16[344,2048]{1,0:T(8,128)(2,1)S(1)} %copy-done.2, bf16[344,2048]{1,0:T(8,128)(2,1)S(1)} %copy-done.2, ...), custom_call_target="tpu_custom_call" | custom-call | tf_op jit(solution)/shard_map/pallas_call | solution.py:123
  33.6 1.5 collective-permute-start.4
  35.9 5.1 %collective-permute-done.5 = bf16[256,768]{1,0:T(8,128)(2,1)S(1)} collective-permute-done((bf16[256,768]{1,0:T(8,128)(2,1)S(1)}, bf16[256,768]{1,0:T(8,128)(2,1)S(1)}, u32[]{:S(2)}, u32[]{:S(2)}) %collective-permute-start.5) | collective-permute-done | bytes 393248 | tf_op jit(solution)/shard_map/g_b/ppermute | solution.py:219
  41.1 2.2 %collective-permute-start.9 = (bf16[256,768]{1,0:T(8,128)(2,1)}, bf16[256,768]{1,0:T(8,128)(2,1)}, u32[]{:S(2)}, u32[]{:S(2)}) collective-permute-start(bf16[256,768]{1,0:T(8,128)(2,1)} %add_convert_fusion.1), channel_id=1, source_target_pairs={{0,16},{4,20},{8,24},{12,28},{16,0},{20,4},{24,8},{28,12},{1,17},{... | collective-permute-start | bytes 1179656 | tf_op jit(solution)/shard_map/d_across/ppermute | solution.py:219
  45.5 1.9 %shard_map.136 = (bf16[2,112,512]{2,1,0:T(8,128)(2,1)}, bf16[2,112,512]{2,1,0:T(8,128)(2,1)}) custom-call(s32[2]{0:T(128)} %pad_add_fusion.place_ref, bf16[112,2048]{1,0:T(8,128)(2,1)} %copy-done.17, bf16[112,1024]{1,0:T(8,128)(2,1)} %copy-done.27), custom_call_target="tpu_custom_call" | custom-call | tf_op jit(solution)/shard_map/pallas_call | solution.py:184
  47.5 2.9 %shard_map.137 = (bf16[256,768]{1,0:T(8,128)(2,1)S(1)}, f32[256,768]{1,0:T(8,128)S(1)}) custom-call(s32[2]{0:T(128)S(1)} %copy-done.14, bf16[344,768]{1,0:T(8,128)(2,1)S(1)} %copy-done.5, bf16[344,768]{1,0:T(8,128)(2,1)} %collective-permute-done.12.refs_1_, bf16[344,2048]{1,0:T(8,128)(2,1)S(1)} %copy-done.2, bf16[344,2048]{1,0:T(8,128)(2,1)S(1)} %copy-done.2, ...), custom_call_target="tpu_custom_call" | custom-call | tf_op jit(solution)/shard_map/pallas_call | solution.py:123
  50.4 3.0 %shard_map.138 = (bf16[256,768]{1,0:T(8,128)(2,1)S(1)}, f32[256,768]{1,0:T(8,128)S(1)}) custom-call(s32[2]{0:T(128)S(1)} %copy-done.14, bf16[344,768]{1,0:T(8,128)(2,1)S(1)} %copy-done.5, bf16[344,768]{1,0:T(8,128)(2,1)} %collective-permute-done.12.refs_1_, bf16[344,2048]{1,0:T(8,128)(2,1)S(1)} %copy-done.2, bf16[344,2048]{1,0:T(8,128)(2,1)S(1)} %copy-done.2, ...), custom_call_target="tpu_custom_call" | custom-call | tf_op jit(solution)/shard_map/pallas_call | solution.py:123
  53.4 1.8 collective-permute-start.13
  56.2 17.6 %collective-permute-done.4 = bf16[256,768]{1,0:T(8,128)(2,1)} collective-permute-done((bf16[256,768]{1,0:T(8,128)(2,1)}, bf16[256,768]{1,0:T(8,128)(2,1)}, u32[]{:S(2)}, u32[]{:S(2)}) %collective-permute-start.4) | collective-permute-done | bytes 393248 | tf_op jit(solution)/shard_map/g_a/ppermute | solution.py:219
  74.5 5.1 %collective-permute-start.17 = (bf16[2,2,112,512]{3,2,1,0:T(8,128)(2,1)S(1)}, bf16[2,2,112,512]{3,2,1,0:T(8,128)(2,1)S(1)}, u32[]{:S(2)}, u32[]{:S(2)}) collective-permute-start(bf16[2,2,112,512]{3,2,1,0:T(8,128)(2,1)S(1)} %pad_maximum_fusion.3), channel_id=1, source_target_pairs={{0,1},{1,3},{3,2},{2,0},{4,5},{5,7},{7,6},{6,4},{8,9},{9,11},{11,1... | collective-permute-start | bytes 1376264 | tf_op jit(solution)/shard_map/rotated/ppermute | solution.py:219
  79.6 2.8 %fusion.42 = (bf16[256,768]{1,0:T(8,128)(2,1)S(1)}, f32[256,768]{1,0:T(8,128)S(1)}, f32[256,768]{1,0:T(8,128)S(1)}, f32[256,768]{1,0:T(8,128)S(1)}, bf16[256,768...) fusion(f32[1,256,3,768]{3,1,2,0:T(8,128)S(1)} %copy-done.18, ...), kind=kLoop, calls=%fused_computation.107 | loop fusion | flops 7864320 | bytes 13369344 | tf_op jit(solution)/shard_map/convert_element_type | solution.py:264
  83.0 3.5 %collective-permute-start.15 = (bf16[256,768]{1,0:T(8,128)(2,1)S(1)}, bf16[256,768]{1,0:T(8,128)(2,1)S(1)}, u32[]{:S(2)}, u32[]{:S(2)}) collective-permute-start(bf16[256,768]{1,0:T(8,128)(2,1)S(1)} %add_convert_fusion), channel_id=1, source_target_pairs={{0,16},{4,20},{8,24},{12,28},{16,0},{20,4},{24,8},{28,12},{1,17},{... | collective-permute-start | bytes 1179656 | tf_op jit(solution)/shard_map/u_across/ppermute | solution.py:219
  86.5 1.5 collective-permute-start.14
  88.0 3.0 %collective-permute-done.17 = bf16[2,2,112,512]{3,2,1,0:T(8,128)(2,1)S(1)} collective-permute-done((bf16[2,2,112,512]{3,2,1,0:T(8,128)(2,1)S(1)}, bf16[2,2,112,512]{3,2,1,0:T(8,128)(2,1)S(1)}, u32[]{:S(2)}, u32[]{:S(2)}) %collective-permute-start.17) | collective-permute-done | bytes 458784 | tf_op jit(solution)/shard_map/rotated/ppermute | solution.py:219
  91.5 5.4 %collective-permute-done.18 = bf16[256,768]{1,0:T(8,128)(2,1)S(1)} collective-permute-done((bf16[256,768]{1,0:T(8,128)(2,1)S(1)}, bf16[256,768]{1,0:T(8,128)(2,1)S(1)}, u32[]{:S(2)}, u32[]{:S(2)}) %collective-permute-start.18) | collective-permute-done | bytes 393248 | tf_op jit(solution)/shard_map/vert_z/ppermute | solution.py:219
  97.5 5.5 %collective-permute-done.19 = bf16[256,768]{1,0:T(8,128)(2,1)S(1)} collective-permute-done((bf16[256,768]{1,0:T(8,128)(2,1)S(1)}, bf16[256,768]{1,0:T(8,128)(2,1)S(1)}, u32[]{:S(2)}, u32[]{:S(2)}) %collective-permute-start.19) | collective-permute-done | bytes 393248 | tf_op jit(solution)/shard_map/g_near/ppermute | solution.py:219
  103.8 4.6 %collective-permute-done.14 = bf16[256,768]{1,0:T(8,128)(2,1)S(1)} collective-permute-done((bf16[256,768]{1,0:T(8,128)(2,1)S(1)}, bf16[256,768]{1,0:T(8,128)(2,1)S(1)}, u32[]{:S(2)}, u32[]{:S(2)}) %collective-permute-start.14) | collective-permute-done | bytes 393248 | tf_op jit(solution)/shard_map/u_a/ppermute | solution.py:219
  110.9 2.5 %collective-permute-start.25 = (bf16[256,768]{1,0:T(8,128)(2,1)S(1)}, bf16[256,768]{1,0:T(8,128)(2,1)S(1)}, u32[]{:S(2)}, u32[]{:S(2)}) collective-permute-start(bf16[256,768]{1,0:T(8,128)(2,1)S(1)} %get-tuple-element.160), channel_id=1, source_target_pairs={{0,16},{4,20},{8,24},{12,28},{16,0},{20,4},{24,8},{28,12},{1,17},{... | collective-permute-start | bytes 1179656 | tf_op jit(solution)/shard_map/d_other/ppermute | solution.py:219
  113.4 12.9 %collective-permute-done.22 = bf16[256,768]{1,0:T(8,128)(2,1)S(1)} collective-permute-done((bf16[256,768]{1,0:T(8,128)(2,1)S(1)}, bf16[256,768]{1,0:T(8,128)(2,1)S(1)}, u32[]{:S(2)}, u32[]{:S(2)}) %collective-permute-start.22) | collective-permute-done | bytes 393248 | tf_op jit(solution)/shard_map/u_near/ppermute | solution.py:219
  127.5 1.5 collective-permute-start.29
  129.4 2.6 %collective-permute-start.26 = (bf16[256,768]{1,0:T(8,128)(2,1)S(1)}, bf16[256,768]{1,0:T(8,128)(2,1)S(1)}, u32[]{:S(2)}, u32[]{:S(2)}) collective-permute-start(bf16[256,768]{1,0:T(8,128)(2,1)S(1)} %collective-permute-done.25), channel_id=1, source_target_pairs={{0,2},{2,0},{1,3},{3,1},{4,6},{6,4},{5,7},{7,5},{8,10},{10,8},{9,1... | collective-permute-start | bytes 1179656 | tf_op jit(solution)/shard_map/vert_f/ppermute | solution.py:219
  132.0 1.6 maximum_bitcast_fusion
  133.6 1.6 maximum_bitcast_fusion.1
  135.5 1.6 maximum_bitcast_fusion.2
  137.1 2.0 %collective-permute-done.29 = bf16[256,768]{1,0:T(8,128)(2,1)S(1)} collective-permute-done((bf16[256,768]{1,0:T(8,128)(2,1)S(1)}, bf16[256,768]{1,0:T(8,128)(2,1)S(1)}, u32[]{:S(2)}, u32[]{:S(2)}) %collective-permute-start.29) | collective-permute-done | bytes 393248 | tf_op jit(solution)/shard_map/hori_z/ppermute | solution.py:219
  139.1 2.9 %collective-permute-done.26 = bf16[256,768]{1,0:T(8,128)(2,1)S(1)} collective-permute-done((bf16[256,768]{1,0:T(8,128)(2,1)S(1)}, bf16[256,768]{1,0:T(8,128)(2,1)S(1)}, u32[]{:S(2)}, u32[]{:S(2)}) %collective-permute-start.26) | collective-permute-done | bytes 393248 | tf_op jit(solution)/shard_map/vert_f/ppermute | solution.py:219
  143.4 5.2 %collective-permute-done.24 = bf16[224,768]{1,0:T(8,128)(2,1)S(1)} collective-permute-done((bf16[224,768]{1,0:T(8,128)(2,1)S(1)}, bf16[224,768]{1,0:T(8,128)(2,1)S(1)}, u32[]{:S(2)}, u32[]{:S(2)}) %collective-permute-start.24) | collective-permute-done | bytes 344096 | tf_op jit(solution)/shard_map/u_grp_got/ppermute | solution.py:219
  148.8 2.9 %collective-permute-done.30 = bf16[256,768]{1,0:T(8,128)(2,1)S(1)} collective-permute-done((bf16[256,768]{1,0:T(8,128)(2,1)S(1)}, bf16[256,768]{1,0:T(8,128)(2,1)S(1)}, u32[]{:S(2)}, u32[]{:S(2)}) %collective-permute-start.30) | collective-permute-done | bytes 393248 | tf_op jit(solution)/shard_map/hori_f/ppermute | solution.py:219
  152.5 2.5 %collective-permute-start.28 = (bf16[112,768]{1,0:T(8,128)(2,1)S(1)}, bf16[112,768]{1,0:T(8,128)(2,1)S(1)}, u32[]{:S(2)}, u32[]{:S(2)}) collective-permute-start(bf16[112,768]{1,0:T(8,128)(2,1)S(1)} %split.85), channel_id=1, source_target_pairs={{0,16},{4,20},{8,24},{12,28},{16,0},{20,4},{24,8},{28,12},{1,17},{... | collective-permute-start | bytes 516104 | tf_op jit(solution)/shard_map/u_far_got/ppermute | solution.py:219
  156.4 7.4 %collective-permute-done.28 = bf16[112,768]{1,0:T(8,128)(2,1)S(1)} collective-permute-done((bf16[112,768]{1,0:T(8,128)(2,1)S(1)}, bf16[112,768]{1,0:T(8,128)(2,1)S(1)}, u32[]{:S(2)}, u32[]{:S(2)}) %collective-permute-start.28) | collective-permute-done | bytes 172064 | tf_op jit(solution)/shard_map/u_far_got/ppermute | solution.py:219
  164.1 1.8 collective-permute-start.33
  166.0 1.7 collective-permute-start.31
  167.8 4.5 %collective-permute-done.34 = bf16[112,768]{1,0:T(8,128)(2,1)S(1)} collective-permute-done((bf16[112,768]{1,0:T(8,128)(2,1)S(1)}, bf16[112,768]{1,0:T(8,128)(2,1)S(1)}, u32[]{:S(2)}, u32[]{:S(2)}) %collective-permute-start.34) | collective-permute-done | bytes 172064 | tf_op jit(solution)/shard_map/near_turned/ppermute | solution.py:219
  173.7 2.6 %convolution_convert_fusion.1 = bf16[112,1024]{1,0:T(8,128)(2,1)S(1)} fusion(bf16[112,768]{1,0:T(8,128)(2,1)S(1)} %collective-permute-done.34, bf16[112,768]{1,0:T(8,128)(2,1)} %collective-permute-done.33, bf16[512,1536]{1,0:T(8,128)(2,1)} %collective-permute-done.32, bf16[256,768]{1,0:T(8,128)(2,1)} %copy-done.24, ...), kind=kOutput, calls=%fused_computation.18 | convolution fusion | flops 368852992 | bytes 3719168 | tf_op jit(solution)/shard_map/dot_general | solution.py:323
  176.9 2.8 %convolution_convert_fusion.2 = bf16[112,1024]{1,0:T(8,128)(2,1)S(1)} fusion(bf16[112,768]{1,0:T(8,128)(2,1)S(1)} %collective-permute-done.31, bf16[112,768]{1,0:T(8,128)(2,1)} %copy-done.28, bf16[512,1536]{1,0:T(8,128)(2,1)} %collective-permute-done.32, bf16[256,768]{1,0:T(8,128)(2,1)S(1)} %copy-done.25, bf16[256,768]{1,0:T(8,128)(2,1)S(1)} %get-tuple-element.196, ...), kind=kOutput, calls=%fused_computation.19 | convolution fusion | flops 368852992 | bytes 3719168 | tf_op jit(solution)/shard_map/dot_general | solution.py:323
  179.7 3.2 %collective-permute-done.35 = bf16[112,1024]{1,0:T(8,128)(2,1)S(1)} collective-permute-done((bf16[112,1024]{1,0:T(8,128)(2,1)S(1)}, bf16[112,1024]{1,0:T(8,128)(2,1)S(1)}, u32[]{:S(2)}, u32[]{:S(2)}) %collective-permute-start.35) | collective-permute-done | bytes 229408 | tf_op jit(solution)/shard_map/near_out_got/ppermute | solution.py:219
  182.9 2.5 %shard_map.139 = bf16[512,2048]{1,0:T(8,128)(2,1)} custom-call(s32[2]{0:T(128)S(1)} %copy-done.14, bf16[512,112]{1,0:T(8,128)(2,1)S(1)} %copy-done.8, f32[512,1]{1,0:T(8,128)S(1)} %copy.20.weight, bf16[112,2048]{1,0:T(8,128)(2,1)S(1)} %pad_maximum_fusion.4.values), custom_call_target="tpu_custom_call" | custom-call | tf_op jit(solution)/shard_map/pallas_call | solution.py:152
  (153 shorter events, 22.6 us)
Async XLA Ops:
  0.6 12.5 %copy-start = (bf16[512,2048]{1,0:T(8,128)(2,1)S(1)}, bf16[512,2048]{1,0:T(8,128)(2,1)}, u32[]{:S(2)}) copy-start(bf16[512,2048]{1,0:T(8,128)(2,1)} %param.17) | copy-start | bytes 6291460
  3.6 7.1 %collective-permute-start.1 = (bf16[344,1024]{1,0:T(8,128)(2,1)}, bf16[344,1024]{1,0:T(8,128)(2,1)}, u32[]{:S(2)}, u32[]{:S(2)}) collective-permute-start(bf16[344,1024]{1,0:T(8,128)(2,1)} %shard_map.130), channel_id=1, source_target_pairs={{0,4},{4,0},{8,12},{12,8},{16,20},{20,16},{24,28},{28,24},{1,5},{5... | collective-permute-start | bytes 2113544 | tf_op jit(solution)/shard_map/cot_got/ppermute | solution.py:219
  7.4 3.3 %collective-permute-start = (bf16[344,768]{1,0:T(8,128)(2,1)}, bf16[344,768]{1,0:T(8,128)(2,1)}, u32[]{:S(2)}, u32[]{:S(2)}) collective-permute-start(bf16[344,768]{1,0:T(8,128)(2,1)} %get-tuple-element.87.refs_0_), channel_id=1, source_target_pairs={{0,4},{4,0},{8,12},{12,8},{16,20},{20,16},{24,28},{28,24},{1,5},{5... | collective-permute-start | bytes 1585160 | tf_op jit(solution)/shard_map/act_got/ppermute | solution.py:219
  14.2 3.6 %collective-permute-start.3 = (bf16[344,1024]{1,0:T(8,128)(2,1)S(1)}, bf16[344,1024]{1,0:T(8,128)(2,1)S(1)}, u32[]{:S(2)}, u32[]{:S(2)}) collective-permute-start(bf16[344,1024]{1,0:T(8,128)(2,1)S(1)} %copy-done.21), channel_id=1, source_target_pairs={{0,4},{4,0},{8,12},{12,8},{16,20},{20,16},{24,28},{28,24},{1,5},{5... | collective-permute-start | bytes 2113544 | tf_op jit(solution)/shard_map/in_got/ppermute | solution.py:219
  14.7 3.1 %collective-permute-start.2 = (bf16[344,768]{1,0:T(8,128)(2,1)S(1)}, bf16[344,768]{1,0:T(8,128)(2,1)S(1)}, u32[]{:S(2)}, u32[]{:S(2)}) collective-permute-start(bf16[344,768]{1,0:T(8,128)(2,1)S(1)} %copy-done.6), channel_id=1, source_target_pairs={{0,4},{4,0},{8,12},{12,8},{16,20},{20,16},{24,28},{28,24},{1,5},{5... | collective-permute-start | bytes 1585160 | tf_op jit(solution)/shard_map/gate_got/ppermute | solution.py:219
  14.9 18.6 %collective-permute-start.6 = (bf16[256,768]{1,0:T(8,128)(2,1)S(1)}, bf16[256,768]{1,0:T(8,128)(2,1)S(1)}, u32[]{:S(2)}, u32[]{:S(2)}) collective-permute-start(bf16[256,768]{1,0:T(8,128)(2,1)S(1)} %shard_map.131), channel_id=1, source_target_pairs={{0,8},{4,12},{8,0},{12,4},{16,24},{20,28},{24,16},{28,20},{1,9},{5... | collective-permute-start | bytes 1179656 | tf_op jit(solution)/shard_map/d_b/ppermute | solution.py:219
  19.4 21.7 %collective-permute-start.5 = (bf16[256,768]{1,0:T(8,128)(2,1)S(1)}, bf16[256,768]{1,0:T(8,128)(2,1)S(1)}, u32[]{:S(2)}, u32[]{:S(2)}) collective-permute-start(bf16[256,768]{1,0:T(8,128)(2,1)S(1)} %get-tuple-element.100), channel_id=1, source_target_pairs={{0,8},{4,12},{8,0},{12,4},{16,24},{20,28},{24,16},{28,20},{1,9},{5... | collective-permute-start | bytes 1179656 | tf_op jit(solution)/shard_map/g_b/ppermute | solution.py:219
  21.8 22.3 %collective-permute-start.10 = (bf16[112,1024]{1,0:T(8,128)(2,1)S(1)}, bf16[112,1024]{1,0:T(8,128)(2,1)S(1)}, u32[]{:S(2)}, u32[]{:S(2)}) collective-permute-start(bf16[112,1024]{1,0:T(8,128)(2,1)S(1)} %constant_dynamic-slice_fusion), channel_id=1, source_target_pairs={{0,16},{4,20},{8,24},{12,28},{16,0},{20,4},{24,8},{28,12},{1,17},{... | collective-permute-start | bytes 688136 | tf_op jit(solution)/shard_map/there/ppermute | solution.py:219
  24.4 23.0 %collective-permute-start.12 = (bf16[344,768]{1,0:T(8,128)(2,1)S(1)}, bf16[344,768]{1,0:T(8,128)(2,1)}, u32[]{:S(2)}, u32[]{:S(2)}) collective-permute-start(bf16[344,768]{1,0:T(8,128)(2,1)S(1)} %copy-done.5), channel_id=1, source_target_pairs={{0,4},{4,0},{8,12},{12,8},{16,20},{20,16},{24,28},{28,24},{1,5},{5... | collective-permute-start | bytes 1585160 | tf_op jit(solution)/shard_map/up_got/ppermute | solution.py:219
  31.0 48.6 %collective-permute-start.8 = (bf16[256,768]{1,0:T(8,128)(2,1)}, bf16[256,768]{1,0:T(8,128)(2,1)}, u32[]{:S(2)}, u32[]{:S(2)}) collective-permute-start(bf16[256,768]{1,0:T(8,128)(2,1)} %get-tuple-element.101), channel_id=1, source_target_pairs={{0,8},{4,12},{8,0},{12,4},{16,24},{20,28},{24,16},{28,20},{1,9},{5... | collective-permute-start | bytes 1179656 | tf_op jit(solution)/shard_map/d_a/ppermute | solution.py:219
  33.5 13.9 %copy-start.14 = (s32[2]{0:T(128)S(1)}, s32[2]{0:T(128)}, u32[]{:S(2)}) copy-start(s32[2]{0:T(128)} %pad_add_fusion.place_ref) | copy-start | bytes 28
  33.6 40.3 %collective-permute-start.4 = (bf16[256,768]{1,0:T(8,128)(2,1)}, bf16[256,768]{1,0:T(8,128)(2,1)}, u32[]{:S(2)}, u32[]{:S(2)}) collective-permute-start(bf16[256,768]{1,0:T(8,128)(2,1)} %get-tuple-element.104), channel_id=1, source_target_pairs={{0,8},{4,12},{8,0},{12,4},{16,24},{20,28},{24,16},{28,20},{1,9},{5... | collective-permute-start | bytes 1179656 | tf_op jit(solution)/shard_map/g_a/ppermute | solution.py:219
  41.1 33.4 %collective-permute-start.9 = (bf16[256,768]{1,0:T(8,128)(2,1)}, bf16[256,768]{1,0:T(8,128)(2,1)}, u32[]{:S(2)}, u32[]{:S(2)}) collective-permute-start(bf16[256,768]{1,0:T(8,128)(2,1)} %add_convert_fusion.1), channel_id=1, source_target_pairs={{0,16},{4,20},{8,24},{12,28},{16,0},{20,4},{24,8},{28,12},{1,17},{... | collective-permute-start | bytes 1179656 | tf_op jit(solution)/shard_map/d_across/ppermute | solution.py:219
  44.8 34.8 %collective-permute-start.7 = (bf16[256,768]{1,0:T(8,128)(2,1)}, bf16[256,768]{1,0:T(8,128)(2,1)}, u32[]{:S(2)}, u32[]{:S(2)}) collective-permute-start(bf16[256,768]{1,0:T(8,128)(2,1)} %add_convert_fusion.2), channel_id=1, source_target_pairs={{0,16},{4,20},{8,24},{12,28},{16,0},{20,4},{24,8},{28,12},{1,17},{... | collective-permute-start | bytes 1179656 | tf_op jit(solution)/shard_map/g_across/ppermute | solution.py:219
  47.4 5.9 %collective-permute-start.11 = (bf16[2,112,512]{2,1,0:T(8,128)(2,1)}, bf16[2,112,512]{2,1,0:T(8,128)(2,1)}, u32[]{:S(2)}, u32[]{:S(2)}) collective-permute-start(bf16[2,112,512]{2,1,0:T(8,128)(2,1)} %get-tuple-element.112), channel_id=1, source_target_pairs={{0,4},{4,0},{8,12},{12,8},{16,20},{20,16},{24,28},{28,24},{1,5},{5... | collective-permute-start | bytes 688136 | tf_op jit(solution)/shard_map/row_got/ppermute | solution.py:219
  47.5 32.1 %copy-start.19 = (f32[1,256,3,768]{3,1,2,0:T(8,128)S(1)}, f32[1,256,3,768]{3,1,2,0:T(8,128)}, u32[]{:S(2)}) copy-start(f32[1,256,3,768]{3,1,2,0:T(8,128)} %param.15) | copy-start | bytes 7077892
  47.5 32.1 %copy-start.20 = (f32[1,256,3,768]{3,1,2,0:T(8,128)S(1)}, f32[1,256,3,768]{3,1,2,0:T(8,128)}, u32[]{:S(2)}) copy-start(f32[1,256,3,768]{3,1,2,0:T(8,128)} %param.16) | copy-start | bytes 7077892
  50.4 29.2 %copy-start.10 = (f32[256,768]{1,0:T(8,128)S(1)}, f32[256,768]{1,0:T(8,128)}, u32[]{:S(2)}) copy-start(f32[256,768]{1,0:T(8,128)} %copy-done.9) | copy-start | bytes 2359300
  50.4 29.2 %copy-start.12 = (f32[256,768]{1,0:T(8,128)S(1)}, f32[256,768]{1,0:T(8,128)}, u32[]{:S(2)}) copy-start(f32[256,768]{1,0:T(8,128)} %copy-done.11) | copy-start | bytes 2359300
  50.4 29.2 %copy-start.18 = (f32[1,256,3,768]{3,1,2,0:T(8,128)S(1)}, f32[1,256,3,768]{3,1,2,0:T(8,128)}, u32[]{:S(2)}) copy-start(f32[1,256,3,768]{3,1,2,0:T(8,128)} %param.14) | copy-start | bytes 7077892
  53.4 29.5 %collective-permute-start.13 = (bf16[256,768]{1,0:T(8,128)(2,1)S(1)}, bf16[256,768]{1,0:T(8,128)(2,1)S(1)}, u32[]{:S(2)}, u32[]{:S(2)}) collective-permute-start(bf16[256,768]{1,0:T(8,128)(2,1)S(1)} %get-tuple-element.116), channel_id=1, source_target_pairs={{0,8},{4,12},{8,0},{12,4},{16,24},{20,28},{24,16},{28,20},{1,9},{5... | collective-permute-start | bytes 1179656 | tf_op jit(solution)/shard_map/u_b/ppermute | solution.py:219
  73.8 12.7 %collective-permute-start.16 = (bf16[2,2,112,512]{3,2,1,0:T(8,128)(2,1)S(1)}, bf16[2,2,112,512]{3,2,1,0:T(8,128)(2,1)S(1)}, u32[]{:S(2)}, u32[]{:S(2)}) collective-permute-start(bf16[2,2,112,512]{3,2,1,0:T(8,128)(2,1)S(1)} %pad_maximum_fusion.3), channel_id=1, source_target_pairs={{0,0},{1,2},{2,1},{3,3},{4,4},{5,6},{6,5},{7,7},{8,8},{9,10},{10,9... | collective-permute-start | bytes 1376264 | tf_op jit(solution)/shard_map/turned/ppermute | solution.py:219
  74.5 16.5 %collective-permute-start.17 = (bf16[2,2,112,512]{3,2,1,0:T(8,128)(2,1)S(1)}, bf16[2,2,112,512]{3,2,1,0:T(8,128)(2,1)S(1)}, u32[]{:S(2)}, u32[]{:S(2)}) collective-permute-start(bf16[2,2,112,512]{3,2,1,0:T(8,128)(2,1)S(1)} %pad_maximum_fusion.3), channel_id=1, source_target_pairs={{0,1},{1,3},{3,2},{2,0},{4,5},{5,7},{7,6},{6,4},{8,9},{9,11},{11,1... | collective-permute-start | bytes 1376264 | tf_op jit(solution)/shard_map/rotated/ppermute | solution.py:219
  82.4 14.5 %collective-permute-start.18 = (bf16[256,768]{1,0:T(8,128)(2,1)S(1)}, bf16[256,768]{1,0:T(8,128)(2,1)S(1)}, u32[]{:S(2)}, u32[]{:S(2)}) collective-permute-start(bf16[256,768]{1,0:T(8,128)(2,1)S(1)} %get-tuple-element.160), channel_id=1, source_target_pairs={{0,2},{2,0},{1,3},{3,1},{4,6},{6,4},{5,7},{7,5},{8,10},{10,8},{9,1... | collective-permute-start | bytes 1179656 | tf_op jit(solution)/shard_map/vert_z/ppermute | solution.py:219
  82.5 20.5 %collective-permute-start.19 = (bf16[256,768]{1,0:T(8,128)(2,1)S(1)}, bf16[256,768]{1,0:T(8,128)(2,1)S(1)}, u32[]{:S(2)}, u32[]{:S(2)}) collective-permute-start(bf16[256,768]{1,0:T(8,128)(2,1)S(1)} %get-tuple-element.123), channel_id=1, source_target_pairs={{0,8},{4,12},{8,0},{12,4},{16,24},{20,28},{24,16},{28,20},{1,9},{5... | collective-permute-start | bytes 1179656 | tf_op jit(solution)/shard_map/g_near/ppermute | solution.py:219
  83.0 20.8 %collective-permute-start.15 = (bf16[256,768]{1,0:T(8,128)(2,1)S(1)}, bf16[256,768]{1,0:T(8,128)(2,1)S(1)}, u32[]{:S(2)}, u32[]{:S(2)}) collective-permute-start(bf16[256,768]{1,0:T(8,128)(2,1)S(1)} %add_convert_fusion), channel_id=1, source_target_pairs={{0,16},{4,20},{8,24},{12,28},{16,0},{20,4},{24,8},{28,12},{1,17},{... | collective-permute-start | bytes 1179656 | tf_op jit(solution)/shard_map/u_across/ppermute | solution.py:219
  86.5 21.9 %collective-permute-start.14 = (bf16[256,768]{1,0:T(8,128)(2,1)S(1)}, bf16[256,768]{1,0:T(8,128)(2,1)S(1)}, u32[]{:S(2)}, u32[]{:S(2)}) collective-permute-start(bf16[256,768]{1,0:T(8,128)(2,1)S(1)} %get-tuple-element.126), channel_id=1, source_target_pairs={{0,8},{4,12},{8,0},{12,4},{16,24},{20,28},{24,16},{28,20},{1,9},{5... | collective-permute-start | bytes 1179656 | tf_op jit(solution)/shard_map/u_a/ppermute | solution.py:219
  103.7 5.4 %collective-permute-start.20 = (bf16[448,768]{1,0:T(8,128)(2,1)S(1)}, bf16[448,768]{1,0:T(8,128)(2,1)S(1)}, u32[]{:S(2)}, u32[]{:S(2)}) collective-permute-start(bf16[448,768]{1,0:T(8,128)(2,1)S(1)} %split.81), channel_id=1, source_target_pairs={{0,4},{4,0},{8,12},{12,8},{16,20},{20,16},{24,28},{28,24},{1,5},{5... | collective-permute-start | bytes 2064392 | tf_op jit(solution)/shard_map/g_core_got/ppermute | solution.py:219
  109.4 17.4 %copy-start.16 = (f32[448,768]{1,0:T(8,128)}, f32[448,768]{1,0:T(8,128)S(1)}, u32[]{:S(2)}) copy-start(f32[448,768]{1,0:T(8,128)S(1)} %convert_add_fusion.1) | copy-start | bytes 4128772
  109.4 16.9 %collective-permute-start.22 = (bf16[256,768]{1,0:T(8,128)(2,1)S(1)}, bf16[256,768]{1,0:T(8,128)(2,1)S(1)}, u32[]{:S(2)}, u32[]{:S(2)}) collective-permute-start(bf16[256,768]{1,0:T(8,128)(2,1)S(1)} %get-tuple-element.148), channel_id=1, source_target_pairs={{0,8},{4,12},{8,0},{12,4},{16,24},{20,28},{24,16},{28,20},{1,9},{5... | collective-permute-start | bytes 1179656 | tf_op jit(solution)/shard_map/u_near/ppermute | solution.py:219
  110.9 18.4 %collective-permute-start.25 = (bf16[256,768]{1,0:T(8,128)(2,1)S(1)}, bf16[256,768]{1,0:T(8,128)(2,1)S(1)}, u32[]{:S(2)}, u32[]{:S(2)}) collective-permute-start(bf16[256,768]{1,0:T(8,128)(2,1)S(1)} %get-tuple-element.160), channel_id=1, source_target_pairs={{0,16},{4,20},{8,24},{12,28},{16,0},{20,4},{24,8},{28,12},{1,17},{... | collective-permute-start | bytes 1179656 | tf_op jit(solution)/shard_map/d_other/ppermute | solution.py:219
  127.4 7.8 %collective-permute-start.23 = (bf16[448,768]{1,0:T(8,128)(2,1)S(1)}, bf16[448,768]{1,0:T(8,128)(2,1)S(1)}, u32[]{:S(2)}, u32[]{:S(2)}) collective-permute-start(bf16[448,768]{1,0:T(8,128)(2,1)S(1)} %split.80), channel_id=1, source_target_pairs={{0,4},{4,0},{8,12},{12,8},{16,20},{20,16},{24,28},{28,24},{1,5},{5... | collective-permute-start | bytes 2064392 | tf_op jit(solution)/shard_map/u_core_got/ppermute | solution.py:219
  127.5 11.5 %collective-permute-start.29 = (bf16[256,768]{1,0:T(8,128)(2,1)S(1)}, bf16[256,768]{1,0:T(8,128)(2,1)S(1)}, u32[]{:S(2)}, u32[]{:S(2)}) collective-permute-start(bf16[256,768]{1,0:T(8,128)(2,1)S(1)} %broadcast_select_fusion.5), channel_id=1, source_target_pairs={{0,1},{1,0},{2,3},{3,2},{4,5},{5,4},{6,7},{7,6},{8,9},{9,8},{10,11... | collective-permute-start | bytes 1179656 | tf_op jit(solution)/shard_map/hori_z/ppermute | solution.py:219
  129.1 19.6 %collective-permute-start.21 = (bf16[224,768]{1,0:T(8,128)(2,1)S(1)}, bf16[224,768]{1,0:T(8,128)(2,1)S(1)}, u32[]{:S(2)}, u32[]{:S(2)}) collective-permute-start(bf16[224,768]{1,0:T(8,128)(2,1)S(1)} %split.83), channel_id=1, source_target_pairs={{0,16},{4,20},{8,24},{12,28},{16,0},{20,4},{24,8},{28,12},{1,17},{... | collective-permute-start | bytes 1032200 | tf_op jit(solution)/shard_map/g_far_got/ppermute | solution.py:219
  129.4 12.6 %collective-permute-start.26 = (bf16[256,768]{1,0:T(8,128)(2,1)S(1)}, bf16[256,768]{1,0:T(8,128)(2,1)S(1)}, u32[]{:S(2)}, u32[]{:S(2)}) collective-permute-start(bf16[256,768]{1,0:T(8,128)(2,1)S(1)} %collective-permute-done.25), channel_id=1, source_target_pairs={{0,2},{2,0},{1,3},{3,1},{4,6},{6,4},{5,7},{7,5},{8,10},{10,8},{9,1... | collective-permute-start | bytes 1179656 | tf_op jit(solution)/shard_map/vert_f/ppermute | solution.py:219
  135.4 13.1 %collective-permute-start.24 = (bf16[224,768]{1,0:T(8,128)(2,1)S(1)}, bf16[224,768]{1,0:T(8,128)(2,1)S(1)}, u32[]{:S(2)}, u32[]{:S(2)}) collective-permute-start(bf16[224,768]{1,0:T(8,128)(2,1)S(1)} %split.82), channel_id=1, source_target_pairs={{0,2},{2,0},{1,3},{3,1},{4,6},{6,4},{5,7},{7,5},{8,10},{10,8},{9,1... | collective-permute-start | bytes 1032200 | tf_op jit(solution)/shard_map/u_grp_got/ppermute | solution.py:219
  137.1 11.6 %slice-start = ((f32[448,768]{1,0:T(8,128)}), f32[224,768]{1,0:T(8,128)S(1)}, s32[]{:S(2)}) async-start(f32[448,768]{1,0:T(8,128)} %copy-done.16), calls=%async_computation | async-start | bytes 1376256 | tf_op jit(solution)/shard_map/split | solution.py:312
  139.0 34.7 %copy-start.23 = (bf16[256,768]{1,0:T(8,128)(2,1)}, bf16[256,768]{1,0:T(8,128)(2,1)S(1)}, u32[]{:S(2)}) copy-start(bf16[256,768]{1,0:T(8,128)(2,1)S(1)} %collective-permute-done.29) | copy-start | bytes 1179652
  142.1 9.6 %collective-permute-start.30 = (bf16[256,768]{1,0:T(8,128)(2,1)S(1)}, bf16[256,768]{1,0:T(8,128)(2,1)S(1)}, u32[]{:S(2)}, u32[]{:S(2)}) collective-permute-start(bf16[256,768]{1,0:T(8,128)(2,1)S(1)} %broadcast_select_fusion.4), channel_id=1, source_target_pairs={{0,1},{1,0},{2,3},{3,2},{4,5},{5,4},{6,7},{7,6},{8,9},{9,8},{10,11... | collective-permute-start | bytes 1179656 | tf_op jit(solution)/shard_map/hori_f/ppermute | solution.py:219
  152.4 21.3 %collective-permute-start.32 = (bf16[512,1536]{1,0:T(8,128)(2,1)S(1)}, bf16[512,1536]{1,0:T(8,128)(2,1)}, u32[]{:S(2)}, u32[]{:S(2)}) collective-permute-start(bf16[512,1536]{1,0:T(8,128)(2,1)S(1)} %maximum_maximum_fusion), channel_id=1, source_target_pairs={{0,4},{4,0},{8,12},{12,8},{16,20},{20,16},{24,28},{28,24},{1,5},{5... | collective-permute-start | bytes 4718600 | tf_op jit(solution)/shard_map/down_got/ppermute | solution.py:219
  152.5 11.4 %collective-permute-start.28 = (bf16[112,768]{1,0:T(8,128)(2,1)S(1)}, bf16[112,768]{1,0:T(8,128)(2,1)S(1)}, u32[]{:S(2)}, u32[]{:S(2)}) collective-permute-start(bf16[112,768]{1,0:T(8,128)(2,1)S(1)} %split.85), channel_id=1, source_target_pairs={{0,16},{4,20},{8,24},{12,28},{16,0},{20,4},{24,8},{28,12},{1,17},{... | collective-permute-start | bytes 516104 | tf_op jit(solution)/shard_map/u_far_got/ppermute | solution.py:219
  155.0 8.9 %collective-permute-start.27 = (bf16[112,768]{1,0:T(8,128)(2,1)S(1)}, bf16[112,768]{1,0:T(8,128)(2,1)S(1)}, u32[]{:S(2)}, u32[]{:S(2)}) collective-permute-start(bf16[112,768]{1,0:T(8,128)(2,1)S(1)} %split.84), channel_id=1, source_target_pairs={{0,2},{2,0},{1,3},{3,1},{4,6},{6,4},{5,7},{7,5},{8,10},{10,8},{9,1... | collective-permute-start | bytes 516104 | tf_op jit(solution)/shard_map/g_grp_got/ppermute | solution.py:219
  164.0 12.4 %copy-start.28 = (bf16[112,768]{1,0:T(8,128)(2,1)}, bf16[112,768]{1,0:T(8,128)(2,1)S(1)}, u32[]{:S(2)}) copy-start(bf16[112,768]{1,0:T(8,128)(2,1)S(1)} %fusion.25) | copy-start | bytes 516100
  164.0 8.3 %collective-permute-start.34 = (bf16[112,768]{1,0:T(8,128)(2,1)S(1)}, bf16[112,768]{1,0:T(8,128)(2,1)S(1)}, u32[]{:S(2)}, u32[]{:S(2)}) collective-permute-start(bf16[112,768]{1,0:T(8,128)(2,1)S(1)} %fusion.25), channel_id=1, source_target_pairs={{0,9},{1,8},{4,13},{5,12},{8,1},{9,0},{12,5},{13,4},{16,25},{17,24... | collective-permute-start | bytes 516104 | tf_op jit(solution)/shard_map/near_turned/ppermute | solution.py:219
  164.1 9.6 %collective-permute-start.33 = (bf16[112,768]{1,0:T(8,128)(2,1)S(1)}, bf16[112,768]{1,0:T(8,128)(2,1)}, u32[]{:S(2)}, u32[]{:S(2)}) collective-permute-start(bf16[112,768]{1,0:T(8,128)(2,1)S(1)} %fusion.25), channel_id=1, source_target_pairs={{0,8},{4,12},{8,0},{12,4},{16,24},{20,28},{24,16},{28,20},{1,9},{5... | collective-permute-start | bytes 516104 | tf_op jit(solution)/shard_map/near_hidden/ppermute | solution.py:219
  166.0 10.9 %copy-start.25 = (bf16[256,768]{1,0:T(8,128)(2,1)S(1)}, bf16[256,768]{1,0:T(8,128)(2,1)}, u32[]{:S(2)}) copy-start(bf16[256,768]{1,0:T(8,128)(2,1)} %copy-done.24) | copy-start | bytes 1179652
  166.0 10.9 %collective-permute-start.31 = (bf16[112,768]{1,0:T(8,128)(2,1)S(1)}, bf16[112,768]{1,0:T(8,128)(2,1)S(1)}, u32[]{:S(2)}, u32[]{:S(2)}) collective-permute-start(bf16[112,768]{1,0:T(8,128)(2,1)S(1)} %fusion.25), channel_id=1, source_target_pairs={{0,1},{1,0},{2,3},{3,2},{4,5},{5,4},{6,7},{7,6},{8,9},{9,8},{10,11... | collective-permute-start | bytes 516104 | tf_op jit(solution)/shard_map/beside/ppermute | solution.py:219
  176.4 6.5 %collective-permute-start.35 = (bf16[112,1024]{1,0:T(8,128)(2,1)S(1)}, bf16[112,1024]{1,0:T(8,128)(2,1)S(1)}, u32[]{:S(2)}, u32[]{:S(2)}) collective-permute-start(bf16[112,1024]{1,0:T(8,128)(2,1)S(1)} %convolution_convert_fusion.1), channel_id=1, source_target_pairs={{0,8},{4,12},{8,0},{12,4},{16,24},{20,28},{24,16},{28,20},{1,9},{5... | collective-permute-start | bytes 688136 | tf_op jit(solution)/shard_map/near_out_got/ppermute | solution.py:219
  (20 other events, 79.5 us)
